TPU v7x, 256 devices: a whole 4x4x8 slice. The times are simulated.
256 devices in a mesh: blk: 16 (over y, x_lo, core), grp: 16 (over z, x_hi).
Axes of the slice: x: 4 (x_hi: 2, x_lo: 2; x = x_hi * 2 + x_lo), y: 4, z: 8, core: 2. Of those that a mesh axis runs over, the one named last changes fastest.
Arguments:
- series: bfloat16 [32768, 2048], P(('blk', 'grp')), may hold values from -24 to 24
- positives: bfloat16 [32768, 256], P(('blk', 'grp')), may hold values from -6 to 6
- w_last: bfloat16 [2048, 4096], P(None, 'grp'), may hold values from -0.125 to 0.125
- w_head: bfloat16 [4096, 256], P('grp'), may hold values from -0.09375 to 0.09375
- pair_index: int32 [32768], P('blk'), may hold values from 0 to 32767, each once
Outputs:
- mean_loss: float32 [], replicated
- grad_last: float32 [2048, 4096], P('blk', 'grp')
- grad_head: float32 [4096, 256], P('grp', 'blk')
Inputs may be any that keep to these rules, and one draw needn't show every extreme that they name: A permutation of the rows: series i is paired with row pair_index[i] of positives.
All inputs are finite; a program needn't handle non-finite values.
Results may differ from a plain program's by a relative error of at most 0.0035.
The roundings to bfloat16 on the way count: a program that leaves them out, or rounds other values in their place, can miss the bound.
Values may be sent and summed in bfloat16 or wider, within the bound.
A program may use at most 64 MiB of HBM per device.

v0:
```python
import jax
import jax.numpy as jnp
from jax import lax
from jax.sharding import PartitionSpec as P

SOFTMAX_TEMP_SCALE = 0.05
EPSILON = 1e-06


def versus_keys(left, right):
    return lax.dot_general(
        left, right, (((1,), (1,)), ((), ())), preferred_element_type=jnp.float32
    )


def through(left, right):
    return lax.dot_general(
        left, right, (((0,), (0,)), ((), ())), preferred_element_type=jnp.float32
    )


def unit_of(head_sum):
    row_norm = jnp.sqrt(jnp.sum(head_sum * head_sum, axis=1, keepdims=True) + EPSILON)
    return (head_sum / row_norm, row_norm)


def on_device(series, positives, w_last, w_head, pair_index):
    tok_dev = series.shape[0]
    member = lax.axis_index("grp")
    members = lax.axis_size("grp")
    group_count = lax.axis_size("blk")
    preact = jnp.dot(
        lax.all_gather(series, "grp", axis=0, tiled=True),
        w_last,
        preferred_element_type=jnp.float32,
    )
    hidden = jax.nn.gelu(preact).astype(jnp.bfloat16)
    head_part = jnp.dot(hidden, w_head, preferred_element_type=jnp.float32)
    key_float = positives.astype(jnp.float32)
    key_norm = jnp.sqrt(jnp.sum(key_float * key_float, axis=1, keepdims=True) + EPSILON)
    unit_key_rows = lax.all_gather(
        (key_float / key_norm).astype(jnp.bfloat16), "blk", axis=0, tiled=True
    )
    owner = pair_index // tok_dev % members
    local_slot = pair_index // (tok_dev * members) * tok_dev + pair_index % tok_dev
    held_keys = jnp.take(unit_key_rows, local_slot, axis=0).astype(jnp.float32)
    matched_part = jnp.where((owner == member)[:, None], held_keys, 0.0)
    matched_scores = lax.psum(matched_part.astype(jnp.bfloat16), "grp").astype(jnp.float32)
    head_sum = lax.psum(head_part, "grp")
    unit_rows, row_norm = unit_of(head_sum)
    query_matrix = unit_rows.astype(jnp.bfloat16)
    group_rows = query_matrix.shape[0]
    block_rows = min(512, group_rows)
    block_count = group_rows // block_rows
    query_blocks = query_matrix.reshape(block_count, block_rows, query_matrix.shape[1])

    def exp_of(query_block):
        return jnp.exp(versus_keys(query_block, unit_key_rows) / SOFTMAX_TEMP_SCALE)

    def weighted_of(exp_terms):
        return jnp.dot(
            exp_terms.astype(jnp.bfloat16), unit_key_rows, preferred_element_type=jnp.float32
        )

    def flatten_rows(values):
        return values.reshape((group_rows,) + values.shape[2:])

    def stat_block(query_block):
        return jnp.sum(exp_of(query_block), axis=1)

    exp_sum = lax.map(stat_block, query_blocks)
    exponent_total = lax.psum(flatten_rows(exp_sum), "grp")
    total_blocks = exponent_total.reshape(block_count, block_rows)

    def grad_block(inputs):
        weighted_keys = weighted_of(exp_of(inputs[0]))
        return weighted_keys / inputs[1][:, None]

    partial_grad = flatten_rows(lax.map(grad_block, (query_blocks, total_blocks)))
    normalized_rows = lax.psum(partial_grad, "grp")
    unit_gradient = (normalized_rows - matched_scores) / SOFTMAX_TEMP_SCALE
    local_query_rows = unit_rows.astype(jnp.bfloat16).astype(jnp.float32)
    positive_total = jnp.sum(local_query_rows * matched_scores, axis=1) / SOFTMAX_TEMP_SCALE
    along = jnp.sum(unit_rows * unit_gradient, axis=1, keepdims=True)
    grad_rows = ((unit_gradient - unit_rows * along) / row_norm).astype(jnp.bfloat16)
    row_loss = jnp.log(exponent_total) - positive_total
    row_loss = lax.dynamic_slice_in_dim(row_loss, member * tok_dev, tok_dev, 0)
    mean_loss = lax.psum(jnp.sum(row_loss), ("blk", "grp")) / (tok_dev * members * group_count)
    d_hidden = versus_keys(grad_rows, w_head)
    pullback = jax.vjp(jax.nn.gelu, preact)[1]
    d_preact = pullback(d_hidden)[0].astype(jnp.bfloat16)
    head_partial = through(hidden, grad_rows)
    last_partial = through(lax.all_gather(series, "grp", axis=0, tiled=True), d_preact)
    grad_last, grad_head = (
        lax.psum_scatter(last_partial, "blk", scatter_dimension=0, tiled=True),
        lax.psum_scatter(head_partial, "blk", scatter_dimension=1, tiled=True),
    )
    return (mean_loss, grad_last, grad_head)


def solution(mesh):
    placed = (
        P(("blk", "grp"), None),
        P(("blk", "grp"), None),
        P(None, "grp"),
        P("grp", None),
        P("blk"),
    )
    return jax.shard_map(
        on_device,
        mesh=mesh,
        in_specs=placed,
        out_specs=(P(), P("blk", "grp"), P("grp", "blk")),
        check_vma=False,
    )
```

profile of v0, /device:TPU:1, one launch (start us, length us, event | category | flops | bytes accessed | tf_op | source)
XLA Modules:
  0.0 830.1 jit_solution(13023591717484984333)
XLA Ops:
  8.0 0.9 fusion.30
  8.9 1.6 fusion.31
  10.6 139.3 %all-gather.3.cloned.1.call-done = bf16[2048,2048]{1,0:T(8,128)(2,1)} async-done(((bf16[128,2048]{1,0:T(8,128)(2,1)}), bf16[2048,2048]{1,0:T(8,128)(2,1)}) %all-gather.3.cloned.1.call-update) | async-done | bytes 8388624 | tf_op jit(solution)/shard_map/all_gather | solution.py:33
  149.8 5.9 fusion.54
  155.7 1.4 copy-done.9
  157.1 2.1 fusion.50
  160.0 24.9 %all-gather.5.cloned.1.call-done = bf16[2048,256]{1,0:T(8,128)(2,1)} async-done(((bf16[128,256]{1,0:T(8,128)(2,1)}), bf16[2048,256]{1,0:T(8,128)(2,1)}) %all-gather.5.cloned.1.call-update) | async-done | bytes 1048592 | tf_op jit(solution)/shard_map/all_gather | solution.py:41
  184.9 8.0 gather_fusion
  192.9 2.5 select_convert_fusion
  195.5 148.5 %all-reduce.4.cloned.1.call-done = f32[2048,256]{1,0:T(8,128)} async-done(((f32[2048,256]{1,0:T(8,128)}), f32[2048,256]{1,0:T(8,128)}) %all-reduce.4.cloned.1.call-update) | async-done | bytes 2097168 | tf_op jit(solution)/shard_map/psum | solution.py:49
  344.0 2.1 multiply_reduce_fusion.1
  347.3 3.6 while.20
  347.3 0.8 exponential_reduce_fusion.2
  348.2 0.8 exponential_reduce_fusion.2
  349.1 0.8 exponential_reduce_fusion.2
  350.0 0.8 exponential_reduce_fusion.2
  350.9 34.3 %psum.36 = f32[2048]{0:T(1024)S(1)} all-reduce(f32[2048]{0:T(1024)S(1)} %bitcast.49), channel_id=1, replica_groups=mesh['blk'=16,'grp'=16] {'grp'}, use_global_device_ids=true, to_apply=%region_6.7 | all-reduce | flops 2048 | bytes 16384 | tf_op jit(solution)/shard_map/psum | solution.py:72
  385.3 8.9 %while.21 = (s32[]{:T(128)}, f32[4,512,256]{2,1,0:T(8,128)}, bf16[4,512,256]{2,1,0:T(8,128)(2,1)S(1)}, bf16[2048,256]{1,0:T(8,128)(2,1)S(1)}, f32[4,512]{1,0:T(4,128)S(1)}, /*index=5*/s32[]{:T(128)}) while((s32[]{:T(128)}, f32[4,512,256]{2,1,0:T(8,128)}, bf16[4,512,256]{2,1,0:T(8,128)(2,1)S(1)}, bf16[2048,256]{1,0:T(8,128)(2,1)S(1)}, ...), condition=%wide.region_12.13_spmd, body=%wide.region_11.12_spmd.sunk | while | flops 1075970048 | bytes 2890825 | solution.py:79
  385.3 2.2 fusion.76
  387.5 2.2 fusion.76
  389.8 2.2 fusion.76
  392.0 2.2 fusion.76
  394.4 109.4 %all-reduce.6.cloned.1.call-done = bf16[2048,256]{1,0:T(8,128)(2,1)} async-done(((bf16[2048,256]{1,0:T(8,128)(2,1)}), bf16[2048,256]{1,0:T(8,128)(2,1)}) %all-reduce.6.cloned.1.call-update) | async-done | bytes 1048592 | tf_op jit(solution)/shard_map/psum | solution.py:48
  503.9 168.1 %all-reduce.8.cloned.1.call-done = f32[2048,256]{1,0:T(8,128)} async-done(((f32[2048,256]{1,0:T(8,128)}), f32[2048,256]{1,0:T(8,128)}) %all-reduce.8.cloned.1.call-update) | async-done | bytes 2097168 | tf_op jit(solution)/shard_map/psum | solution.py:80
  672.0 3.1 multiply_reduce_fusion
  675.1 1.6 divide_convert_fusion
  676.7 9.5 %convolution_bitcast_fusion = f32[2048,256]{0,1:T(8,128)} fusion(bf16[2048,2048]{1,0:T(8,128)(2,1)} %all-gather.3.cloned.1.call-done, f32[2048,256]{1,0:T(8,128)} %copy-done.9, bf16[2048,256]{1,0:T(8,128)(2,1)} %divide_convert_fusion, bf16[256,256]{1,0:T(8,128)(2,1)S(1)} %copy-done.8), kind=kOutput, calls=%fused_computation.17 | convolution fusion | flops 2426404864 | bytes 13762560 | tf_op jit(solution)/shard_map/dot_general | solution.py:17
  686.3 1.1 copy-done.6
  687.4 3.3 fusion.49
  691.4 84.7 %psum.38 = f32[]{:T(128)} all-reduce(f32[]{:T(128)} %fusion.42), channel_id=1, replica_groups=mesh['blk'=16,'grp'=16] {'blk','grp'}, use_global_device_ids=true, to_apply=%region_10.11 | all-reduce | flops 1 | bytes 8 | tf_op jit(solution)/shard_map/psum | solution.py:88
  776.8 1.7 copy.8
  778.5 43.6 %reduce-scatter.5.cloned.1.call-done = f32[256,16]{0,1:T(8,128)} async-done(((f32[256,256]{0,1:T(8,128)}), f32[256,16]{0,1:T(8,128)}) %reduce-scatter.5.cloned.1.call-update) | async-done | bytes 16400 | tf_op jit(solution)/shard_map/reduce_scatter | solution.py:96
  (51 shorter events, 4.1 us)
Async XLA Ops:
  7.2 142.7 %copy-start = (bf16[2048,256]{1,0:T(8,128)(2,1)S(1)}, bf16[2048,256]{1,0:T(8,128)(2,1)}, u32[]{:S(2)}) copy-start(bf16[2048,256]{1,0:T(8,128)(2,1)} %param.11) | copy-start | bytes 3145732
  7.2 142.7 %all-gather.3.cloned.1.call-start = ((), (), s32[]{:S(2)}) async-start(), calls=%async_computation.2 | async-start | bytes 8912896 | tf_op jit(solution)/shard_map/all_gather | solution.py:33
  7.9 177.0 %all-gather.5.cloned.1.call-start = ((), (), s32[]{:S(2)}) async-start(), calls=%async_computation.4 | async-start | bytes 1114112 | tf_op jit(solution)/shard_map/all_gather | solution.py:41
  10.5 146.6 %copy-start.8 = (bf16[256,256]{1,0:T(8,128)(2,1)S(1)}, bf16[256,256]{1,0:T(8,128)(2,1)}, u32[]{:S(2)}) copy-start(bf16[256,256]{1,0:T(8,128)(2,1)} %param.12) | copy-start | bytes 393220
  10.5 333.4 %all-reduce.4.cloned.1.call-start = ((), (), s32[]{:S(2)}) async-start(), calls=%async_computation.3 | async-start | bytes 4194304 | tf_op jit(solution)/shard_map/psum | solution.py:49
  155.7 1.4 copy-start.9
  159.2 0.7 copy-start.7
  159.3 344.6 %all-reduce.6.cloned.1.call-start = ((), (), s32[]{:S(2)}) async-start(), calls=%async_computation.5 | async-start | bytes 2097152 | tf_op jit(solution)/shard_map/psum | solution.py:48
  195.4 476.6 %all-reduce.8.cloned.1.call-start = ((), (), s32[]{:S(2)}) async-start(), calls=%async_computation.6 | async-start | bytes 4194304 | tf_op jit(solution)/shard_map/psum | solution.py:80
  344.0 2.2 copy-start.2
  346.1 1.3 copy-start.1
  394.2 277.8 %copy-start.3 = (f32[2048,256]{1,0:T(8,128)S(1)}, f32[2048,256]{1,0:T(8,128)}, u32[]{:S(2)}) copy-start(f32[2048,256]{1,0:T(8,128)} %all-reduce.4.cloned.1.call-done) | copy-start | bytes 6291460
  394.2 382.6 %reduce-scatter.3.cloned.1.call-start = ((), (), s32[]{:S(2)}) async-start(), calls=%async_computation.7 | async-start | bytes 2228224 | tf_op jit(solution)/shard_map/reduce_scatter | solution.py:95
  672.0 3.1 copy-start.4
  672.0 3.1 copy-start.5
  686.2 1.2 copy-start.6
  686.2 135.9 %reduce-scatter.5.cloned.1.call-start = ((), (), s32[]{:S(2)}) async-start(), calls=%async_computation.8 | async-start | bytes 278528 | tf_op jit(solution)/shard_map/reduce_scatter | solution.py:96
Sparse Core Ops, SparseCore 0:
  10.6 139.1 all-gather.2
  152.3 32.5 all-gather.4
  187.6 156.3 all-reduce.3
  346.4 157.3 all-reduce.5
  506.5 165.4 all-reduce.7
  686.3 71.2 reduce-scatter.2
  760.9 61.2 reduce-scatter.4
where the time goes:
time: 833 us; the launch traced here: 830 us
  waiting for transfers between devices  635 us (76%)
  blocking collectives  119 us (14%)
  matrix products  33 us (4%)
  between operations  16.1 us (2%)
  local copies, waits for them, and re-layouts  13.9 us (2%)
  other arithmetic  12.8 us (2%)
    psum x1, waiting for transfers between devices, on_device(): normalized_rows = lax.psum(partial_grad, 'grp')  168 us
    psum x1, waiting for transfers between devices, on_device(): head_sum = lax.psum(head_part, 'grp')  148 us
    all_gather x1, waiting for transfers between devices, on_device(): lax.all_gather(series, 'grp', axis=0, tiled=True)  139 us
    psum x1, waiting for transfers between devices, on_device(): lax.psum(matched_part.astype(jnp.bfloat16), 'grp').astype(jnp.float32)  109 us
    psum x1, blocking collectives, on_device(): lax.psum(jnp.sum(row_loss), ('blk', 'grp'))  84.7 us
    reduce_scatter x1, waiting for transfers between devices, on_device(): lax.psum_scatter(head_partial, 'blk', scatter_dimension=1, tiled=True)  43.6 us
    psum x1, blocking collectives, on_device(): exponent_total = lax.psum(flatten_rows(exp_sum), 'grp')  34.3 us
    all_gather x1, waiting for transfers between devices, on_device(): lax.all_gather((key_float / key_norm).astype(jnp.bfloat16), 'blk', axis=0...  24.9 us
  transfers between devices with their start and end apart: 7, of which 6 were waited for; matrix products, arithmetic and copies ran while one was open for 5% of the time, Pallas kernels for 0%

commit v1 on v0

v1 whole, which is shorter than its diff:
```python
import math
import types

import jax
import jax.numpy as jnp
from jax import lax
from jax.experimental import pallas as pl
from jax.experimental.pallas import tpu as pltpu
from jax.sharding import PartitionSpec as P

MESH = pl.DeviceIdType.MESH
F32 = jnp.float32
BF16 = jnp.bfloat16

TEMP = 0.05
EPSILON = 1e-06
GELU_A = math.sqrt(2.0 / math.pi)
GELU_B = 0.044715
VMEM_BYTES = 56 * 1024 * 1024


def dot_nn(left, right):
    return lax.dot_general(left, right, (((1,), (0,)), ((), ())), preferred_element_type=F32)


def dot_nt(left, right):
    return lax.dot_general(left, right, (((1,), (1,)), ((), ())), preferred_element_type=F32)


def fold_lanes(x):
    total = x[:, 0:128]
    for k in range(1, x.shape[1] // 128):
        total = total + x[:, k * 128 : (k + 1) * 128]
    return total


def kernel(dims, refs_in, refs_out, refs):
    Z, PL, TB, D, HS, E, TOKENS = dims
    series, positives, w_last, w_head, pair = refs_in
    loss_out, gl_out, gh_out = refs_out
    r = refs
    U = PL // 2
    HALF = TB // 2
    UNIT = 2 * TB
    KEYS = 2 * Z * TB
    DS = D // PL
    ES = E // PL
    GRP_ROWS = 2 * Z * TB
    J = Z - 1
    blk = lax.axis_index("blk")
    grp = lax.axis_index("grp")
    core = blk % 2
    other = 1 - core
    xhi = grp % 2
    z = grp // 2
    uid = blk // 2
    pid = uid * 2 + xhi
    sib_dev = (uid * 2 + other, grp)
    holder = core == xhi

    def zwrap(v):
        return lax.rem(v + 2 * Z, Z)

    def column(zz):
        return (blk, zz * 2 + xhi)

    def plane(p):
        return ((p // 2) * 2 + core, z * 2 + p % 2)

    def rows_of(zz, c, start=0, size=TB):
        return pl.ds(pl.multiple_of((zz * 2 + c) * TB + start, 16), size)

    def unit_rows_of(u):
        return pl.ds(pl.multiple_of(u * UNIT, UNIT), UNIT)

    def remote(src, dst, ssem, rsem, dev):
        return pltpu.make_async_remote_copy(
            src_ref=src, dst_ref=dst, send_sem=ssem, recv_sem=rsem, device_id=dev, device_id_type=MESH
        )

    def each(low, high, body):
        def step(i, c):
            body(i)
            return c

        lax.fori_loop(low, high, step, 0)

    def unit_z(i):
        half = (i + 1) // 2
        return zwrap(z + half * (1 - 2 * (i % 2)))

    def unit_u(i):
        total = 0
        for b in range(U.bit_length() - 1):
            mine, flip = (uid // (1 << b)) % 2, (i // (1 << b)) % 2
            total = total + (mine + flip - 2 * mine * flip) * (1 << b)
        return total

    barrier = pltpu.get_barrier_semaphore()

    def greet(dev):
        pl.semaphore_signal(barrier, inc=1, device_id=dev, device_id_type=MESH)

    def greet_plane(i):
        p = lax.rem(pid + i, PL)
        greet(plane(p))
        greet(((p // 2) * 2 + xhi, z * 2 + p % 2))

    greet(sib_dev)
    each(1, Z, lambda i: greet(column(zwrap(z + i))))
    each(1, PL, greet_plane)

    own_rows = rows_of(z, core)
    x_copy = pltpu.make_async_copy(series, r.xbuf.at[own_rows], r.x_sem)
    x_copy.start()
    key_float = positives[...].astype(F32)
    key_norm = jnp.sqrt(jnp.sum(key_float * key_float, axis=1, keepdims=True) + EPSILON)
    r.kbuf[own_rows, :] = (key_float / key_norm).astype(BF16)
    r.prbuf[uid] = pair[...]

    pl.semaphore_wait(barrier, 1 + (Z - 1) + (PL - 1) + PL - 2 * jnp.where(holder, 1, 0))

    def key_zz(direction, s):
        return zwrap(z - s) if direction == 0 else zwrap(z + s)

    def key_hops(direction):
        return Z // 2 - direction

    def key_copy(direction, s):
        rows = rows_of(key_zz(direction, s), core)
        dev = column(zwrap(z + 1 - 2 * direction))
        return remote(
            r.kbuf.at[rows], r.kbuf.at[rows], r.k_send.at[direction, s], r.k_recv.at[direction, s], dev
        )

    def key_arrival(direction, s):
        rows = rows_of(key_zz(direction, s), core)
        return remote(
            r.kbuf.at[rows], r.kbuf.at[rows], r.k_send.at[direction, s - 1], r.k_recv.at[direction, s - 1], sib_dev
        )

    def key_sib(direction, s, c):
        rows = rows_of(key_zz(direction, s), c)
        return remote(
            r.kbuf.at[rows], r.kbuf.at[rows], r.ks_send.at[direction, s], r.ks_recv.at[direction, s], sib_dev
        )

    def key_pass(s):
        for direction in (0, 1):
            if s <= key_hops(direction):
                key_arrival(direction, s).wait_recv()
                if s < key_hops(direction):
                    key_copy(direction, s).start()
                key_sib(direction, s, core).start()

    for direction in (0, 1):
        if key_hops(direction) > 0:
            key_copy(direction, 0).start()
    key_sib(0, 0, core).start()

    def ring_rows(direction, j, hops, c):
        s = j // 2 + hops
        h = j % 2 if direction == 0 else 1 - j % 2
        zz = zwrap(z - s) if direction == 0 else zwrap(z + s)
        return rows_of(zz, c, h * HALF, HALF), h

    def ring_copy(direction, j):
        rows, h = ring_rows(direction, j, 0, core)
        src = series.at[pl.ds(h * HALF, HALF)] if j < 2 else r.xbuf.at[rows]
        dev = column(zwrap(z + 1 - 2 * direction))
        return remote(src, r.xbuf.at[rows], r.ring_send.at[direction, j], r.ring_recv.at[direction, j], dev)

    def arrived(direction, j, c, ssem, rsem):
        rows, _ = ring_rows(direction, j, 1, c)
        return remote(r.xbuf.at[rows], r.xbuf.at[rows], ssem.at[direction, j], rsem.at[direction, j], sib_dev)

    def ring_arrival(direction, j):
        return arrived(direction, j, core, r.ring_send, r.ring_recv)

    def sib_copy(direction, j):
        return arrived(direction, j, core, r.sib_send, r.sib_recv)

    def sib_arrival(direction, j):
        return arrived(direction, j, other, r.sib_send, r.sib_recv)

    for j in range(min(2, J)):
        for direction in (0, 1):
            ring_copy(direction, j).start()
    own_copy = remote(series, r.xbuf.at[own_rows], r.own_send, r.own_recv, sib_dev)
    own_copy.start()

    partner = (blk, z * 2 + 1 - xhi)
    w_copies = [
        remote(w_last, r.wbuf, r.w_send.at[0], r.w_recv.at[0], partner),
        remote(w_head, r.whbuf, r.w_send.at[1], r.w_recv.at[1], partner),
    ]

    @pl.when(holder)
    def _():
        for copy in w_copies:
            copy.start()
        pltpu.make_async_copy(w_last, r.wbuf, r.w_recv.at[0]).start()
        pltpu.make_async_copy(w_head, r.whbuf, r.w_recv.at[1]).start()

    def pair_copy(i):
        u = lax.rem(uid + i, U)
        return remote(pair, r.prbuf.at[uid], r.pr_send.at[i], r.pr_recv.at[uid], plane(u * 2 + xhi))

    def pair_arrival(i):
        u = lax.rem(uid + i, U)
        return remote(pair, r.prbuf.at[u], r.pr_send.at[i], r.pr_recv.at[u], sib_dev)

    each(1, U, lambda i: pair_copy(i).start())

    def to_owner(buf, dst, ssem, rsem, p):
        return remote(buf.at[p], dst.at[pid], ssem.at[p], rsem.at[pid], plane(p))

    def from_helper(buf, dst, ssem, rsem, i):
        p = lax.rem(pid + i, PL)
        return remote(buf.at[p], dst.at[p], ssem.at[p], rsem.at[p], sib_dev)

    m_ops = (r.msend, r.mrecv, r.m_send, r.m_recv)

    def send_unit(u, ops):
        for b in (0, 1):
            p = u * 2 + b

            @pl.when(p != pid)
            def _():
                to_owner(*ops, p).start()

    def find_pairs(i):
        u = unit_u(i)
        lanes = lax.broadcasted_iota(jnp.int32, (UNIT, TB), 1)
        both = [jnp.broadcast_to(r.prbuf[u, pl.ds(z * 2 + b, 1), :], (TB, TB)).T for b in (0, 1)]
        both = jnp.concatenate(both, axis=0) - lanes
        total = jnp.zeros((UNIT, E), F32)
        for zz in range(Z):
            base = (blk - core) * GRP_ROWS + (zz * 2 + xhi) * TB
            hot = jnp.concatenate([both == base, both == base + GRP_ROWS], axis=1)
            hot = jnp.where(hot, 1.0, 0.0).astype(BF16)
            total = total + dot_nn(hot, r.kbuf[zz * UNIT : (zz + 1) * UNIT, :])
        for b in (0, 1):
            r.msend[u * 2 + b] = total[b * TB : (b + 1) * TB, :].astype(BF16)
        send_unit(u, m_ops)

    def hs_copy(zz):
        return remote(r.hsend.at[zz], r.hsib.at[zz], r.hs_send.at[zz], r.hs_recv.at[zz], sib_dev)

    def hd_copy(zz):
        return remote(r.hdir.at[zz], r.hrecv.at[z], r.hd_send.at[zz], r.hd_recv.at[z], column(zz))

    def hd_arrival(zz):
        return remote(r.hdir.at[zz], r.hrecv.at[zz], r.hd_send.at[zz], r.hd_recv.at[zz], sib_dev)

    def encode(i):
        zz = unit_z(i)
        rows = unit_rows_of(zz)
        x = dot_nn(r.xbuf[rows, :], r.wbuf[...])
        x2 = x * x
        t = jnp.tanh(GELU_A * (x + GELU_B * (x2 * x)))
        cdf = 0.5 + 0.5 * t
        hidden = (x * cdf).astype(BF16)
        r.hid[rows, :] = hidden
        r.dgelu[rows, :] = cdf + (0.5 * GELU_A) * x * (1.0 - t * t) * (1.0 + (3.0 * GELU_B) * x2)
        r.hp[rows, :] = dot_nn(hidden, r.whbuf[...])
        r.hsend[zz] = r.hp[rows_of(zz, other), :]
        hs_copy(zz).start()

    def head_send(i):
        zz = unit_z(i)
        hs_copy(zz).wait_recv()
        r.hdir[zz] = (r.hp[rows_of(zz, core), :] + r.hsib[zz]).astype(BF16)
        hd_copy(zz).start()

    x_copy.wait()
    key_pass(1)
    key_pass(2)
    for j in range(J):
        for direction in (0, 1):
            ring_arrival(direction, j).wait_recv()
            if j + 2 < J:
                ring_copy(direction, j + 2).start()
            sib_copy(direction, j).start()
        s = j // 2
        if j == 0:
            for k in range(3, Z // 2 + 1):
                key_pass(k)
        elif j == 1:
            each(1, U, lambda i: pair_arrival(i).wait_recv())
            for direction in (0, 1):
                for k in range(direction, key_hops(direction) + 1):
                    key_sib(direction, k, other).wait_recv()
            each(0, U // 2, find_pairs)
        elif j % 2 == 0:
            if j == 2:
                remote(series, r.xbuf.at[rows_of(z, other)], r.own_send, r.own_recv, sib_dev).wait_recv()
                w_copies[0].wait_recv()
                w_copies[1].wait_recv()
            for direction in (0, 1):
                sib_arrival(direction, j - 2).wait_recv()
                sib_arrival(direction, j - 1).wait_recv()
            each(2 * s - 1 if s > 1 else 0, 2 * s + 1, encode)
        else:
            each(2 * s - 1, 2 * s + 1, head_send)
            if j == 3:
                each(U // 2, U, find_pairs)
    for direction in (0, 1):
        sib_arrival(direction, J - 1).wait_recv()
    encode(Z - 1)
    each(Z - 3, Z, head_send)

    hs_copy(z).wait_recv()
    head = r.hp[own_rows, :] + r.hsib[z]
    for i in range(1, Z):
        zz = zwrap(z + i)
        hd_arrival(zz).wait_recv()
        head = head + r.hrecv[zz].astype(F32)
    row_norm = jnp.sqrt(jnp.sum(head * head, axis=1, keepdims=True) + EPSILON)
    unit_rows = head / row_norm
    r.ubuf[...] = unit_rows
    r.rnbuf[...] = jnp.broadcast_to(row_norm, (TB, 128))
    r.qbuf[pid] = unit_rows.astype(BF16)

    def q_copy(p):
        return remote(r.qbuf.at[pid], r.qbuf.at[pid], r.q_send.at[p], r.q_recv.at[pid], plane(p))

    def q_arrival(p):
        return remote(r.qbuf.at[p], r.qbuf.at[p], r.q_send.at[p], r.q_recv.at[p], sib_dev)

    def each_piece(i, body):
        u = unit_u(i)
        for b in (0, 1):
            p = u * 2 + b

            @pl.when(p != pid)
            def _():
                body(p)

    each(0, U, lambda i: each_piece(i, lambda p: q_copy(p).start()))

    CHUNK = min(512, KEYS)
    scale = (1.0 / TEMP) * math.log2(math.e)
    p_ops = (r.psend, r.precv, r.p_send, r.p_recv)
    t_ops = (r.tsend, r.trecv, r.t_send, r.t_recv)

    def attend(i):
        u = unit_u(i)
        each_piece(i, lambda p: q_arrival(p).wait_recv())
        q = r.qbuf[pl.ds(u * 2, 2)].reshape(UNIT, E)
        total = jnp.zeros((UNIT, 128), F32)
        weighted = jnp.zeros((UNIT, E), F32)
        for k in range(KEYS // CHUNK):
            keys = r.kbuf[k * CHUNK : (k + 1) * CHUNK, :]
            e = jnp.exp2(dot_nt(q, keys) * scale)
            total = total + fold_lanes(e)
            weighted = weighted + dot_nn(e.astype(BF16), keys)
        for b in (0, 1):
            part = jnp.sum(total[b * TB : (b + 1) * TB, :].T, axis=0, keepdims=True)
            r.tsend[u * 2 + b] = jnp.broadcast_to(part, (8, TB))
            r.psend[u * 2 + b] = weighted[b * TB : (b + 1) * TB, :].astype(BF16)
        send_unit(u, p_ops)
        send_unit(u, t_ops)

    each(0, U, attend)

    weighted = r.psend[pid].astype(F32)
    totals = r.tsend[pid]
    matched = r.msend[pid].astype(F32)
    for i in range(1, PL):
        p = lax.rem(pid + i, PL)
        from_helper(*m_ops, i).wait_recv()
        matched = matched + r.mrecv[p].astype(F32)
    for i in range(1, PL):
        p = lax.rem(pid + i, PL)
        from_helper(*p_ops, i).wait_recv()
        from_helper(*t_ops, i).wait_recv()
        weighted = weighted + r.precv[p].astype(F32)
        totals = totals + r.trecv[p]

    inv = jnp.broadcast_to(1.0 / totals[0:1, :], (128, TB)).T
    grad = (weighted * jnp.concatenate([inv] * (E // 128), axis=1) - matched) * (1.0 / TEMP)
    unit_rows = r.ubuf[...]
    along = jnp.sum(unit_rows * grad, axis=1, keepdims=True)
    norm = jnp.concatenate([r.rnbuf[...]] * (E // 128), axis=1)
    r.gbuf[own_rows, :] = ((grad - unit_rows * along) / norm).astype(BF16)

    def g_direct(i):
        rows = r.gbuf.at[own_rows]
        return remote(rows, rows, r.gd_send.at[i], r.gd_recv.at[z], column(unit_z(i)))

    def g_direct_arrival(i):
        zz = unit_z(i)
        rows = r.gbuf.at[rows_of(zz, core)]
        return remote(rows, rows, r.gd_send.at[i], r.gd_recv.at[zz], sib_dev)

    def g_sibling(i, c):
        zz = unit_z(i)
        rows = r.gbuf.at[rows_of(zz, c)]
        return remote(rows, rows, r.gs_send.at[zz], r.gs_recv.at[zz], sib_dev)

    g_sibling(0, core).start()
    each(1, Z, lambda i: g_direct(i).start())

    hit = r.qbuf[pid].astype(F32) * matched
    hit = fold_lanes(jnp.sum(hit.reshape(TB // 8, 8, E), axis=0))
    first = lax.broadcasted_iota(jnp.int32, (8, TB), 0) == 0
    r.lplane[pid] = jnp.where(first, jnp.log(totals), 0.0) - hit * (1.0 / TEMP)

    def lp_copy(i):
        rows = r.lplane.at[pid]
        return remote(rows, rows, r.lp_send.at[i], r.lp_recv.at[pid], plane(lax.rem(pid + i, PL)))

    def lp_arrival(i):
        p = lax.rem(pid + i, PL)
        return remote(r.lplane.at[p], r.lplane.at[p], r.lp_send.at[i], r.lp_recv.at[p], sib_dev)

    def lc_copy(i):
        rows = r.lcol.at[z]
        return remote(rows, rows, r.lc_send.at[i], r.lc_recv.at[z], column(zwrap(z + i)))

    def lc_arrival(i):
        zz = zwrap(z + i)
        return remote(r.lcol.at[zz], r.lcol.at[zz], r.lc_send.at[i], r.lc_recv.at[zz], sib_dev)

    def ls_copy(c):
        return remote(r.lsib.at[c], r.lsib.at[c], r.ls_send, r.ls_recv, sib_dev)

    each(1, PL, lambda i: lp_copy(i).start())

    r.ghacc[...] = jnp.zeros((E, HS), F32)

    def back(i):
        @pl.when(i + 1 < Z)
        def _():
            g_direct_arrival(i + 1).wait_recv()
            g_sibling(i + 1, core).start()

        g_sibling(i, other).wait_recv()
        rows = unit_rows_of(unit_z(i))
        g = r.gbuf[rows, :]
        dp = dot_nt(g, r.whbuf[...]) * r.dgelu[rows, :]
        r.dpt[:, rows] = dp.T.astype(BF16)
        gt = g.astype(F32).T.astype(BF16)
        r.ghacc[...] += dot_nn(gt, r.hid[rows, :])

    each(0, Z, back)
    r.ghb[...] = r.ghacc[...].astype(BF16)

    each(1, PL, lambda i: lp_arrival(i).wait_recv())
    loss = r.lplane[0]
    for p in range(1, PL):
        loss = loss + r.lplane[p]
    r.lcol[z] = loss
    each(1, Z, lambda i: lc_copy(i).start())

    def f_copy(d):
        return remote(r.fsend.at[d], r.frecv.at[pid], r.f_send.at[d], r.f_recv.at[pid], (d, z * 2 + core))

    def f_arrival(p):
        return remote(r.frecv.at[p], r.frecv.at[p], r.f_send.at[p], r.f_recv.at[p], sib_dev)

    def last(i):
        n = unit_u(U - 1 - i)
        cols = pl.ds(pl.multiple_of(n * 2 * DS, 2 * DS), 2 * DS)
        part = dot_nn(r.dpt[...], r.xbuf[:, cols]).astype(BF16)
        for k in (0, 1):
            d = n * 2 + k
            r.fsend[d, 0:HS, :] = part[:, k * DS : (k + 1) * DS]
            gh = r.ghb[pl.ds(pl.multiple_of(d * ES, 16), ES), :]
            for c in range(HS // 128):
                r.fsend[d, HS + c * ES : HS + (c + 1) * ES, :] = gh[:, c * 128 : (c + 1) * 128]
            local = jnp.logical_and(holder, d == blk)

            @pl.when(jnp.logical_not(local))
            def _():
                f_copy(d).start()

            @pl.when(local)
            def _():
                pltpu.make_async_copy(r.fsend.at[d], r.frecv.at[pid], r.f_recv.at[pid]).start()

    each(0, U, last)

    each(1, Z, lambda i: lc_arrival(i).wait_recv())
    loss = r.lcol[0]
    for p in range(1, Z):
        loss = loss + r.lcol[p]
    r.lsib[core] = loss
    ls_copy(core).start()

    for direction in (0, 1):
        for j in range(J):
            ring_copy(direction, j).wait_send()
            sib_copy(direction, j).wait_send()
        for s in range(key_hops(direction)):
            key_copy(direction, s).wait_send()
        for s in range(direction, key_hops(direction) + 1):
            key_sib(direction, s, core).wait_send()
    own_copy.wait_send()

    @pl.when(holder)
    def _():
        for copy in w_copies:
            copy.wait_send()

    each(1, U, lambda i: pair_copy(i).wait_send())
    each(0, Z, lambda i: hs_copy(i).wait_send())
    each(1, Z, lambda i: hd_copy(unit_z(i)).wait_send())

    def sent(i):
        p = lax.rem(pid + i, PL)
        q_copy(p).wait_send()
        to_owner(*m_ops, p).wait_send()
        to_owner(*p_ops, p).wait_send()
        to_owner(*t_ops, p).wait_send()
        lp_copy(i).wait_send()

    each(1, PL, sent)
    each(0, Z, lambda i: g_sibling(i, core).wait_send())
    each(1, Z, lambda i: g_direct(i).wait_send())
    each(1, Z, lambda i: lc_copy(i).wait_send())

    each(0, PL, lambda i: f_arrival(i).wait_recv())
    total = r.frecv[0].astype(F32)
    for p in range(1, PL):
        total = total + r.frecv[p].astype(F32)
    gl_out[...] = total[0:HS, :].T
    gh = jnp.concatenate([total[HS + c * ES : HS + (c + 1) * ES, :] for c in range(HS // 128)], axis=1)
    pad = jnp.concatenate([gh, jnp.zeros((128 - ES, HS), F32)], axis=0) if ES < 128 else gh
    gh_out[...] = pad.T[:, 0:ES]

    ls_copy(other).wait_recv()
    ls_copy(core).wait_send()
    loss = r.lsib[0] + r.lsib[1]
    loss = jnp.sum(loss, axis=1, keepdims=True)
    loss = jnp.sum(loss, axis=0, keepdims=True) * (1.0 / TOKENS)
    loss_out[...] = jnp.broadcast_to(loss, (8, 128))

    def f_sent(d):
        @pl.when(jnp.logical_not(jnp.logical_and(holder, d == blk)))
        def _():
            f_copy(d).wait_send()

    each(0, PL, f_sent)


def solution(mesh):
    PL = mesh.shape["blk"]
    Z = mesh.shape["grp"] // 2
    M = 2 * Z

    def on_device(series, positives, w_last, w_head, pair_index):
        TB, D = series.shape
        HS = w_last.shape[1]
        E = w_head.shape[1]
        J = Z - 1
        DS, ES = D // PL, E // PL
        dims = (Z, PL, TB, D, HS, E, TB * PL * M)
        pair = pair_index.reshape(M, TB)
        vm, sem = pltpu.VMEM, pltpu.SemaphoreType.DMA
        rows = M * TB
        fr = HS + ES * (HS // 128)
        scratch = dict(
            xbuf=vm((rows, D), BF16),
            wbuf=vm((D, HS), BF16),
            whbuf=vm((HS, E), BF16),
            kbuf=vm((rows, E), BF16),
            prbuf=vm((PL // 2, M, TB), jnp.int32),
            msend=vm((PL, TB, E), BF16),
            mrecv=vm((PL, TB, E), BF16),
            hid=vm((rows, HS), BF16),
            dgelu=vm((rows, HS), F32),
            hp=vm((rows, E), F32),
            hsend=vm((Z, TB, E), F32),
            hsib=vm((Z, TB, E), F32),
            hdir=vm((Z, TB, E), BF16),
            hrecv=vm((Z, TB, E), BF16),
            ubuf=vm((TB, E), F32),
            rnbuf=vm((TB, 128), F32),
            qbuf=vm((PL, TB, E), BF16),
            psend=vm((PL, TB, E), BF16),
            precv=vm((PL, TB, E), BF16),
            tsend=vm((PL, 8, TB), F32),
            trecv=vm((PL, 8, TB), F32),
            gbuf=vm((rows, E), BF16),
            dpt=vm((HS, rows), BF16),
            ghacc=vm((E, HS), F32),
            ghb=vm((E, HS), BF16),
            fsend=vm((PL, fr, DS), BF16),
            frecv=vm((PL, fr, DS), BF16),
            lplane=vm((PL, 8, 128), F32),
            lcol=vm((Z, 8, 128), F32),
            lsib=vm((2, 8, 128), F32),
            x_sem=sem,
            own_send=sem,
            own_recv=sem,
            ls_send=sem,
            ls_recv=sem,
        )
        for name, shape in dict(
            ring=(2, J), sib=(2, J), k=(2, Z // 2 + 1), ks=(2, Z // 2 + 1), w=(2,), pr=(PL // 2,), m=(PL,),
            hs=(Z,), hd=(Z,), q=(PL,), p=(PL,), t=(PL,), gd=(Z,), gs=(Z,), lp=(PL,), lc=(Z,), f=(PL,),
        ).items():
            scratch[name + "_send"] = sem(shape)
            scratch[name + "_recv"] = sem(shape)
        names = list(scratch)

        def body(*refs):
            kernel(dims, refs[:5], refs[5:8], types.SimpleNamespace(**dict(zip(names, refs[8:]))))

        any_spec = pl.BlockSpec(memory_space=pl.ANY)
        vm_spec = pl.BlockSpec(memory_space=pltpu.VMEM)
        loss, grad_last, grad_head = pl.pallas_call(
            body,
            out_shape=(
                jax.ShapeDtypeStruct((8, 128), F32),
                jax.ShapeDtypeStruct((DS, HS), F32),
                jax.ShapeDtypeStruct((HS, ES), F32),
            ),
            in_specs=[any_spec, vm_spec, any_spec, any_spec, vm_spec],
            out_specs=(vm_spec, vm_spec, vm_spec),
            scratch_shapes=list(scratch.values()),
            compiler_params=pltpu.CompilerParams(
                collective_id=0, has_side_effects=True, vmem_limit_bytes=VMEM_BYTES
            ),
        )(series, positives, w_last, w_head, pair)
        return (loss[0, 0], grad_last, grad_head)

    return jax.shard_map(
        on_device,
        mesh=mesh,
        in_specs=(
            P(("blk", "grp"), None),
            P(("blk", "grp"), None),
            P(None, "grp"),
            P("grp", None),
            P("blk"),
        ),
        out_specs=(P(), P("blk", "grp"), P("grp", "blk")),
        check_vma=False,
    )
```

time: 833 us -> 155 us (0.19)
  waiting for transfers between devices: 635 us -> 0 us
  Pallas kernels: 0 us -> 150 us
  blocking collectives: 119 us -> 0 us
  matrix products: 33 us -> 0 us
  between operations: 16.1 us -> 0.65 us
  other arithmetic: 12.8 us -> 0 us
  local copies, waits for them, and re-layouts: 13.9 us -> 3.47 us
    psum x3 -> x0, waiting for transfers between devices: 426 us -> none  [the longest x1 168 us: on_device(): normalized_rows = lax.psum(partial_grad, 'grp')]
    all_gather x2 -> x0, waiting for transfers between devices: 164 us -> none  [the longest x1 139 us: on_device(): lax.all_gather(series, 'grp', axis=0, tiled=True)]
    pallas_call x0 -> x1, Pallas kernels: none -> 150 us  [on_device(): pl.pallas_call(body, out_shape=(jax.ShapeDtypeStruct((8, 128), F32), jax....]
    psum x2 -> x0, blocking collectives: 119 us -> none  [the longest x1 84.7 us: on_device(): lax.psum(jnp.sum(row_loss), ('blk', 'grp'))]
    reduce_scatter x2 -> x0, waiting for transfers between devices: 43.6 us -> none  [the longest x1 43.6 us: on_device(): lax.psum_scatter(head_partial, 'blk', scatter_dimension=1, tiled=True)]
    dot_general x12 -> x0, matrix products: 33 us -> none  [the longest x2 12.8 us: through(): lax.dot_general(left, right, (((0,), (0,)), ((), ())), preferred_element_...]
  transfers between devices with their start and end apart: 7 -> 0, of which waited for: 6 -> 0; matrix products, arithmetic and copies ran while one was open for 5% -> 0% of each run, Pallas kernels for 0% -> 0%
where the time goes in v1:
time: 155 us
  Pallas kernels  150 us (97%)
  local copies, waits for them, and re-layouts  3.47 us (2%)
    pallas_call x1, Pallas kernels, on_device(): pl.pallas_call(body, out_shape=(jax.ShapeDtypeStruct((8, 128), F32), jax....  150 us

profile of v1, /device:TPU:1, one launch (start us, length us, event | category | flops | bytes accessed | tf_op | source)
XLA Modules:
  0.0 154.6 jit_solution(7054067320407611137)
XLA Ops:
  0.6 150.4 %shard_map.76 = (f32[8,128]{1,0:T(8,128)}, f32[128,256]{1,0:T(8,128)}, f32[256,16]{1,0:T(8,128)}) custom-call(bf16[128,2048]{1,0:T(8,128)(2,1)} %refs_0_.1, bf16[128,256]{1,0:T(8,128)(2,1)} %refs_1_.1, bf16[2048,256]{1,0:T(8,128)(2,1)} %refs_2_.1, bf16[256,256]{1,0:T(8,128)(2,1)} %refs_3_.1, s32[16,128]{1,0:T(8,128)} %bitcast.2), custom_call_target="tpu_custom_call" | custom-call | tf_op jit(solution)/shard_map/pallas_call | solution.py:614
  151.1 0.0 copy-start
  151.1 1.2 slice.3
  152.3 1.6 %copy.8 = f32[256,16]{0,1:T(8,128)} copy(f32[256,16]{1,0:T(8,128)} %get-tuple-element.11) | data formatting | bytes 32768
  153.9 0.0 copy-done
  153.9 0.7 copy.10
Async XLA Ops:
  151.1 2.8 %copy-start = (f32[128,256]{1,0:T(8,128)S(1)}, f32[128,256]{1,0:T(8,128)}, u32[]{:S(2)}) copy-start(f32[128,256]{1,0:T(8,128)} %get-tuple-element.16) | copy-start | bytes 393220

commit v2 on v0

v2 whole, which is shorter than its diff:
```python
import functools
import math
import types

import jax
import jax.numpy as jnp
from jax import lax
from jax.experimental import pallas as pl
from jax.experimental.pallas import tpu as pltpu
from jax.sharding import PartitionSpec as P

MESH = pl.DeviceIdType.MESH
F32 = jnp.float32
BF16 = jnp.bfloat16

TEMP = 0.05
EPSILON = 1e-06
GELU_A = math.sqrt(2.0 / math.pi)
GELU_B = 0.044715
KEY_CHUNKS = 2
CHUNKS = (2, 4)
VMEM_BYTES = 56 * 1024 * 1024


def dot_nn(left, right):
    return lax.dot_general(left, right, (((1,), (0,)), ((), ())), preferred_element_type=F32)


def dot_nt(left, right):
    return lax.dot_general(left, right, (((1,), (1,)), ((), ())), preferred_element_type=F32)


def fold_lanes(x):
    total = x[:, 0:128]
    for k in range(1, x.shape[1] // 128):
        total = total + x[:, k * 128 : (k + 1) * 128]
    return total


def kernel(dims, refs_in, refs_out, refs):
    Z, PL, TB, D, HS, E, TOKENS = dims
    series, positives, w_last, w_head, pair = refs_in
    loss_out, gl_out, gh_out = refs_out
    r = refs
    U = PL // 2
    HOPS = Z // 2
    PT = TB // 2
    PART = 2 * Z * PT
    QUAD = 4 * PT
    KEYS = 2 * Z * TB
    DS = D // PL
    ES = E // PL
    GRP_ROWS = 2 * Z * TB
    blk = lax.axis_index("blk")
    grp = lax.axis_index("grp")
    core = blk % 2
    xhi = grp % 2
    z = grp // 2
    uid = blk // 2
    pid = uid * 2 + xhi
    sib_blk = uid * 2 + 1 - core
    sib_dev = (sib_blk, grp)
    holder = core == xhi

    UB = U.bit_length() - 1
    ubits = [(uid // (1 << b)) % 2 for b in range(UB)]

    def flip(bit, by):
        if isinstance(by, int):
            return 1 - bit if by else bit
        return bit + by - 2 * bit * by

    def bits_of(j, count):
        if isinstance(j, int):
            return [(j >> b) & 1 for b in range(count)]
        out = []
        for b in reversed(range(count)):
            bit = jnp.where(j >= (1 << b), 1, 0)
            out.append(bit)
            j = j - bit * (1 << b)
        return out[::-1]

    def unit_z(i):
        t = z + ((i + 1) // 2) * (1 - 2 * (i % 2))
        return jnp.where(t < 0, t + Z, jnp.where(t >= Z, t - Z, t))

    def column(i):
        return (blk, unit_z(i) * 2 + xhi)

    def seen_from(i):
        return i if i in (0, Z - 1) else (i + 1 if i % 2 else i - 1)

    def unit_of(flips):
        return sum(flip(bit, by) * (1 << b) for b, (bit, by) in enumerate(zip(ubits, flips)))

    def unit_u(j):
        return unit_of(bits_of(j, UB))

    def plane(i, b=None):
        if b is None:
            b, i = i % 4, i // 4
        u = unit_of([b // 2] + bits_of(i, UB - 1))
        return (u * 2 + core, z * 2 + flip(xhi, b % 2))

    def remote(src, dst, ssem, rsem, dev):
        return pltpu.make_async_remote_copy(
            src_ref=src, dst_ref=dst, send_sem=ssem, recv_sem=rsem, device_id=dev, device_id_type=MESH
        )

    def each(low, high, body):
        def step(i, c):
            body(i)
            return c

        lax.fori_loop(low, high, step, 0)

    barrier = pltpu.get_barrier_semaphore()

    def greet(dev):
        pl.semaphore_signal(barrier, inc=1, device_id=dev, device_id_type=MESH)

    greet(sib_dev)
    for i in range(1, Z):
        greet(column(i))
    for i in range(1, PL):
        greet(plane(i))
        greet((unit_u(i // 2) * 2 + xhi, z * 2 + flip(xhi, i % 2)))

    own_copies = [
        pltpu.make_async_copy(series.at[pl.ds(k * PT, PT)], r.xbuf.at[pl.ds(k * PART, PT)], r.x_sem.at[k])
        for k in (0, 1)
    ]
    for copy in own_copies:
        copy.start()
    key_float = positives[...].astype(F32)
    key_norm = jnp.sqrt(jnp.sum(key_float * key_float, axis=1, keepdims=True) + EPSILON)
    r.kbuf[0:TB, :] = (key_float / key_norm).astype(BF16)
    r.prbuf[0] = pair[...]

    pl.semaphore_wait(barrier, 1 + (Z - 1) + (PL - 1) + PL - 2 * jnp.where(holder, 1, 0))

    class Ring:
        def __init__(self, name, buf, base, rows, chunks, source):
            self.buf, self.base, self.rows, self.chunks, self.source = buf, base, rows, chunks, source
            self.sems = [getattr(r, name + s) for s in ("_send", "_recv", "s_send", "s_recv")]

        def place(self, direction, hop):
            return 0 if hop == 0 else min(2 * hop - 1 + direction, Z - 1)

        def chunk_list(self, direction, hop):
            half = self.chunks // 2
            if hop == HOPS:
                return list(range(half)) if direction == 0 else list(range(half, self.chunks))
            order = list(range(self.chunks))
            return order if direction == 0 else order[half:] + order[:half]

        def at(self, i, rel, chunk, count=1):
            size = self.rows // self.chunks
            return self.buf.at[pl.ds(self.base + (i * 2 + rel) * self.rows + chunk * size, size * count)]

        def send(self, direction, hop, chunk):
            size = self.rows // self.chunks
            src = self.at(self.place(direction, hop), 0, chunk)
            if hop == 0 and self.source is not None:
                src = self.source.at[pl.ds(chunk * size, size)]
            k = hop * self.chunks + chunk
            return remote(
                src,
                self.at(self.place(direction, hop + 1), 0, chunk),
                self.sems[0].at[direction, k],
                self.sems[1].at[direction, k],
                column(1 + (1 - direction)),
            )

        def arrival(self, direction, hop, chunk):
            ref = self.at(self.place(direction, hop), 0, chunk)
            k = (hop - 1) * self.chunks + chunk
            return remote(ref, ref, self.sems[0].at[direction, k], self.sems[1].at[direction, k], sib_dev)

        def over(self, direction, hop, chunk, rel=0):
            i = self.place(direction, hop)
            k = (hop - 1) * self.chunks + chunk
            src = self.at(i, rel, chunk)
            return remote(
                src, self.at(i, 1, chunk), self.sems[2].at[direction, k], self.sems[3].at[direction, k], sib_dev
            )

        def over_own(self, rel=0):
            src = self.at(0, rel, 0, self.chunks)
            if rel == 0 and self.source is not None:
                src = self.source
            last = HOPS * self.chunks - self.chunks // 2 - 1 + self.chunks
            return remote(
                src, self.at(0, 1, 0, self.chunks), self.sems[2].at[0, last], self.sems[3].at[0, last], sib_dev
            )

        def begin(self):
            for a, b in zip(self.chunk_list(0, 0), self.chunk_list(1, 0)):
                self.send(0, 0, a).start()
                self.send(1, 0, b).start()
            self.over_own().start()

        def passing(self, hop, n):
            for direction in (0, 1):
                chunk = self.chunk_list(direction, hop)[n]
                self.arrival(direction, hop, chunk).wait_recv()
                if hop + 1 <= HOPS and chunk in self.chunk_list(direction, hop + 1):
                    self.send(direction, hop, chunk).start()
                self.over(direction, hop, chunk).start()

        def passing_all(self, hop):
            for n in range(len(self.chunk_list(0, hop))):
                self.passing(hop, n)

        def other_ready(self, hop):
            for direction in (0, 1) if hop else ():
                for chunk in self.chunk_list(direction, hop):
                    self.over(direction, hop, chunk, 1).wait_recv()
            if hop == 0:
                self.over_own(1).wait_recv()

        def drain(self):
            for direction in (0, 1):
                for hop in range(HOPS + 1):
                    for chunk in self.chunk_list(direction, hop):
                        if hop < HOPS and chunk in self.chunk_list(direction, hop + 1):
                            self.send(direction, hop, chunk).wait_send()
                        if hop:
                            self.over(direction, hop, chunk).wait_send()
            self.over_own().wait_send()

    keys_ring = Ring("k", r.kbuf, 0, TB, KEY_CHUNKS, None)
    rings = [
        Ring("ab"[k], r.xbuf, k * PART, PT, CHUNKS[k], series.at[pl.ds(k * PT, PT)]) for k in (0, 1)
    ]
    keys_ring.begin()
    rings[0].begin()

    partner = (blk, z * 2 + 1 - xhi)
    w_copies = [
        remote(w_last, r.wbuf, r.w_send.at[0], r.w_recv.at[0], partner),
        remote(w_head, r.whbuf, r.w_send.at[1], r.w_recv.at[1], partner),
    ]

    @pl.when(holder)
    def _():
        for copy in w_copies:
            copy.start()
        pltpu.make_async_copy(w_last, r.wbuf, r.w_recv.at[0]).start()
        pltpu.make_async_copy(w_head, r.whbuf, r.w_recv.at[1]).start()

    def pair_copy(j):
        return remote(pair, r.prbuf.at[j], r.pr_send.at[j], r.pr_recv.at[j], plane(j * 2))

    for j in range(1, U):
        pair_copy(j).start()

    class Swap:
        def __init__(self, name, src, dst, part):
            self.src, self.dst = src.at[part], dst.at[part]
            self.ssem, self.rsem = (getattr(r, name + s).at[part] for s in ("_send", "_recv"))

        def copy(self, i, b=None):
            k = i if b is None else i * 4 + b
            return remote(self.src.at[k], self.dst.at[k], self.ssem.at[k], self.rsem.at[k], plane(i, b))

        def own_copy(self, i, b=None):
            k = i if b is None else i * 4 + b
            return remote(self.src.at[0], self.dst.at[k], self.ssem.at[k], self.rsem.at[k], plane(i, b))

    swap_m = [Swap("m", r.msend, r.mrecv, k) for k in (0, 1)]
    swap_q = [Swap("q", r.qbuf, r.qbuf, k) for k in (0, 1)]
    swap_p = [Swap("p", r.psend, r.precv, k) for k in (0, 1)]
    swap_t = [Swap("t", r.tsend, r.trecv, k) for k in (0, 1)]

    def quad(u, body):
        for b in range(4):
            if b == 0:
                pl.when(u != 0)(functools.partial(body, u, b))
            else:
                body(u, b)

    def find_pairs(k):
        def unit(u):
            lanes = lax.broadcasted_iota(jnp.int32, (QUAD, TB), 1)
            cols = []
            for b in range(4):
                row = r.prbuf[u * 2 + b // 2, pl.ds(z * 2 + flip(xhi, b % 2), 1), :]
                cols.append(jnp.broadcast_to(row, (TB, TB)).T[k * PT : (k + 1) * PT, :])
            both = jnp.concatenate(cols, axis=0) - lanes
            total = jnp.zeros((QUAD, E), F32)
            for i in range(Z):
                low = (unit_z(i) * 2 + xhi) * TB
                hot = jnp.concatenate([both == blk * GRP_ROWS + low, both == sib_blk * GRP_ROWS + low], axis=1)
                hot = jnp.where(hot, 1.0, 0.0).astype(BF16)
                total = total + dot_nn(hot, r.kbuf[i * 2 * TB : (i + 1) * 2 * TB, :])
            for b in range(4):
                r.msend[k, u * 4 + b] = total[b * PT : (b + 1) * PT, :].astype(BF16)
            quad(u, lambda *at: swap_m[k].copy(*at).start())

        each(0, PL // 4, unit)

    def block(hop):
        return (0, 1) if hop == 0 else (2 * hop - 1, min(2 * hop + 1, Z))

    def hs_copy(k, i):
        return remote(r.hsend.at[k, i], r.hsib.at[k, i], r.hs_send.at[k, i], r.hs_recv.at[k, i], sib_dev)

    def hd_copy(k, i):
        slot = seen_from(i)
        return remote(r.hdir.at[k, i], r.hrecv.at[k, slot], r.hd_send.at[k, i], r.hd_recv.at[k, slot], column(i))

    def encode(k, hop):
        rings[k].other_ready(hop)
        low, high = block(hop)
        start, stop = k * PART + low * 2 * PT, k * PART + high * 2 * PT
        x = dot_nn(r.xbuf[start:stop, :], r.wbuf[...])
        x2 = x * x
        t = jnp.tanh(GELU_A * (x + GELU_B * (x2 * x)))
        cdf = 0.5 + 0.5 * t
        hidden = x * cdf
        out = dot_nn(hidden.astype(BF16), r.whbuf[...])
        for i in range(low, high):
            first = (i - low) * 2 * PT
            r.hown[k, i] = out[first : first + PT, :]
            r.hsend[k, i] = out[first + PT : first + 2 * PT, :]
            hs_copy(k, i).start()
        r.hidt[:, start:stop] = hidden.T.astype(BF16)
        dgelu = cdf + (0.5 * GELU_A) * x * (1.0 - t * t) * (1.0 + (3.0 * GELU_B) * x2)
        r.dgt[:, start:stop] = dgelu.T

    def head_send(k, hop):
        for i in range(*block(hop)):
            if i:
                hs_copy(k, i).wait_recv()
                r.hdir[k, i] = (r.hown[k, i] + r.hsib[k, i]).astype(BF16)
                hd_copy(k, i).start()

    def make_queries(k):
        hs_copy(k, 0).wait_recv()
        head = r.hown[k, 0] + r.hsib[k, 0]
        for i in range(1, Z):
            hd_copy(k, seen_from(i)).wait_recv()
            head = head + r.hrecv[k, i].astype(F32)
        row_norm = jnp.sqrt(jnp.sum(head * head, axis=1, keepdims=True) + EPSILON)
        unit_rows = head / row_norm
        r.ubuf[k] = unit_rows
        r.rnbuf[k] = jnp.broadcast_to(row_norm, (PT, 128))
        r.qbuf[k, 0] = unit_rows.astype(BF16)
        for i in range(1, PL):
            swap_q[k].own_copy(i).start()

    CHUNK = min(512, KEYS)
    scale = (1.0 / TEMP) * math.log2(math.e)

    def attend(k):
        def unit(u):
            quad(u, lambda *at: swap_q[k].own_copy(*at).wait_recv())
            q = r.qbuf[k, pl.ds(u * 4, 4)].reshape(QUAD, E)
            total = jnp.zeros((QUAD, 128), F32)
            weighted = jnp.zeros((QUAD, E), F32)
            for c in range(KEYS // CHUNK):
                keys = r.kbuf[c * CHUNK : (c + 1) * CHUNK, :]
                e = jnp.exp2(dot_nt(q, keys) * scale)
                total = total + fold_lanes(e)
                weighted = weighted + dot_nn(e.astype(BF16), keys)
            for b in range(4):
                r.psend[k, u * 4 + b] = weighted[b * PT : (b + 1) * PT, :].astype(BF16)
            for b in (0, 1):
                part = jnp.sum(total[b * 2 * PT : (b + 1) * 2 * PT, :].T, axis=0, keepdims=True)
                part = jnp.broadcast_to(part, (8, 2 * PT))
                r.tsend[k, u * 4 + b * 2] = part
                r.tsend[k, u * 4 + b * 2 + 1] = part
            quad(u, lambda *at: swap_p[k].copy(*at).start())
            quad(u, lambda *at: swap_t[k].copy(*at).start())

        each(0, PL // 4, unit)

    def g_rows(k, i, rel):
        return r.gbuf.at[pl.ds(k * PART + (i * 2 + rel) * PT, PT)]

    def g_direct(k, i):
        slot = seen_from(i)
        return remote(g_rows(k, 0, 0), g_rows(k, slot, 0), r.gd_send.at[k, i], r.gd_recv.at[k, slot], column(i))

    def g_arrival(k, i):
        ref = g_rows(k, i, 0)
        return remote(ref, ref, r.gd_send.at[k, i], r.gd_recv.at[k, i], sib_dev)

    def g_over(k, i, rel=0):
        return remote(g_rows(k, i, rel), g_rows(k, i, 1), r.gs_send.at[k, i], r.gs_recv.at[k, i], sib_dev)

    def make_rows(k):
        matched = r.msend[k, 0].astype(F32)
        for i in range(1, PL):
            swap_m[k].copy(i).wait_recv()
            matched = matched + r.mrecv[k, i].astype(F32)
        weighted = r.psend[k, 0].astype(F32)
        totals = [r.tsend[k, 0], jnp.zeros((8, 2 * PT), F32)]
        for i in range(1, PL):
            swap_p[k].copy(i).wait_recv()
            swap_t[k].copy(i).wait_recv()
            weighted = weighted + r.precv[k, i].astype(F32)
            totals[i % 2] = totals[i % 2] + r.trecv[k, i]
        sides = [jnp.broadcast_to(totals[b][0:1, :], (128, 2 * PT)).T for b in (0, 1)]
        total = sides[0][0:PT, :] + sides[1][PT : 2 * PT, :]
        wide = jnp.concatenate([total] * (E // 128), axis=1)
        grad = (weighted / wide - matched) * (1.0 / TEMP)
        unit_rows = r.ubuf[k]
        along = jnp.sum(unit_rows * grad, axis=1, keepdims=True)
        norm = jnp.concatenate([r.rnbuf[k]] * (E // 128), axis=1)
        r.gbuf[k * PART : k * PART + PT, :] = ((grad - unit_rows * along) / norm).astype(BF16)
        g_over(k, 0).start()
        for i in range(1, Z):
            g_direct(k, i).start()
        hit = r.qbuf[k, 0].astype(F32) * matched
        hit = fold_lanes(jnp.sum(hit.reshape(PT // 8, 8, E), axis=0))
        logs = jnp.sum(jnp.log(total).reshape(PT // 8, 8, 128), axis=0)
        first = lax.broadcasted_iota(jnp.int32, (8, 128), 1) == 0
        return jnp.where(first, logs, 0.0) - hit * (1.0 / TEMP)

    def back(k):
        for hop in range(HOPS + 1):
            low, high = block(hop)
            for i in range(low, high):
                if i:
                    g_arrival(k, i).wait_recv()
                    g_over(k, i).start()
            for i in range(low, high):
                g_over(k, i, 1).wait_recv()
            start, stop = k * PART + low * 2 * PT, k * PART + high * 2 * PT
            dp = dot_nt(r.whbuf[...], r.gbuf[start:stop, :]) * r.dgt[:, start:stop]
            r.dpt[:, start:stop] = dp.astype(BF16)

    def lp_copy(i):
        return remote(r.lplane.at[pid], r.lplane.at[pid], r.lp_send.at[i], r.lp_recv.at[i], plane(i))

    def lp_arrival(i):
        p = unit_u(i // 2) * 2 + flip(xhi, i % 2)
        return remote(r.lplane.at[p], r.lplane.at[p], r.lp_send.at[i], r.lp_recv.at[i], sib_dev)

    def lc_copy(i):
        ref = r.lcol.at[z]
        return remote(ref, ref, r.lc_send.at[i], r.lc_recv.at[seen_from(i)], column(i))

    def lc_arrival(i):
        ref = r.lcol.at[unit_z(i)]
        return remote(ref, ref, r.lc_send.at[i], r.lc_recv.at[i], sib_dev)

    def ls_copy(c):
        return remote(r.lsib.at[c], r.lsib.at[c], r.ls_send, r.ls_recv, sib_dev)

    for copy in own_copies:
        copy.wait()
    for hop in range(1, HOPS):
        keys_ring.passing_all(hop)
        rings[0].passing_all(hop)
    rings[1].begin()
    for copy in w_copies:
        copy.wait_recv()
    for hop in range(HOPS - 1):
        encode(0, hop)
    for j in range(1, U):
        pair_copy(j).wait_recv()
    keys_ring.passing_all(HOPS)
    rings[0].passing_all(HOPS)
    encode(0, HOPS - 1)
    encode(0, HOPS)
    for hop in range(1, HOPS - 1):
        head_send(0, hop)
    rings[1].passing(1, 0)
    head_send(0, HOPS - 1)
    head_send(0, HOPS)
    for n in range(1, CHUNKS[1]):
        rings[1].passing(1, n)
    for hop in range(HOPS + 1):
        keys_ring.other_ready(hop)
    find_pairs(0)
    rings[1].passing_all(2)
    make_queries(0)
    find_pairs(1)
    rings[1].passing_all(3)
    encode(1, 0)
    attend(0)
    encode(1, 1)
    rings[1].passing_all(4)
    encode(1, 2)
    encode(1, 3)
    encode(1, 4)
    for hop in range(1, HOPS + 1):
        head_send(1, hop)
    loss = make_rows(0)
    make_queries(1)
    back(0)
    attend(1)
    loss = loss + make_rows(1)
    r.lplane[pid] = loss
    for i in range(1, PL):
        lp_copy(i).start()
    back(1)

    ghead = dot_nn(r.hidt[...], r.gbuf[...])
    r.ghb[...] = ghead.T.astype(BF16)

    for i in range(1, PL):
        lp_arrival(i).wait_recv()
    loss = r.lplane[0]
    for p in range(1, PL):
        loss = loss + r.lplane[p]
    r.lcol[z] = loss
    for i in range(1, Z):
        lc_copy(i).start()

    def f_copy(j, c):
        slot = j * 2 + jnp.where(holder, 0, 1)
        return remote(
            r.fsend.at[j, c],
            r.frecv.at[slot],
            r.f_send.at[j, c],
            r.f_recv.at[slot],
            (unit_u(j) * 2 + c, z * 2 + core),
        )

    def f_local(j, c):
        return jnp.logical_and(jnp.logical_and(holder, j == 0), c == core)

    def last(step):
        j = U - 1 - step
        n = unit_u(j)
        cols = pl.ds(pl.multiple_of(n * 2 * DS, 2 * DS), 2 * DS)
        part = dot_nn(r.dpt[...], r.xbuf[:, cols]).astype(BF16)
        for c in (0, 1):
            d = n * 2 + c
            r.fsend[j, c, 0:HS, :] = part[:, c * DS : (c + 1) * DS]
            gh = r.ghb[pl.ds(pl.multiple_of(d * ES, 16), ES), :]
            for w in range(HS // 128):
                r.fsend[j, c, HS + w * ES : HS + (w + 1) * ES, :] = gh[:, w * 128 : (w + 1) * 128]

            @pl.when(jnp.logical_not(f_local(j, c)))
            def _():
                f_copy(j, c).start()

            @pl.when(f_local(j, c))
            def _():
                pltpu.make_async_copy(r.fsend.at[j, c], r.frecv.at[0], r.f_recv.at[0]).start()

    each(0, U, last)

    for i in range(1, Z):
        lc_arrival(i).wait_recv()
    loss = r.lcol[0]
    for p in range(1, Z):
        loss = loss + r.lcol[p]
    r.lsib[core] = loss
    ls_copy(core).start()

    for ring in [keys_ring] + rings:
        ring.drain()

    @pl.when(holder)
    def _():
        for copy in w_copies:
            copy.wait_send()

    for j in range(1, U):
        pair_copy(j).wait_send()
    for k in (0, 1):
        for i in range(Z):
            hs_copy(k, i).wait_send()
            g_over(k, i).wait_send()
            if i:
                hd_copy(k, i).wait_send()
                g_direct(k, i).wait_send()
        for i in range(1, PL):
            swap_q[k].own_copy(i).wait_send()
            swap_m[k].copy(i).wait_send()
            swap_p[k].copy(i).wait_send()
            swap_t[k].copy(i).wait_send()
    for i in range(1, PL):
        lp_copy(i).wait_send()
    for i in range(1, Z):
        lc_copy(i).wait_send()

    ls_copy(1 - core).wait_recv()
    ls_copy(core).wait_send()
    loss = r.lsib[0] + r.lsib[1]
    loss = jnp.sum(loss, axis=1, keepdims=True)
    loss_out[...] = jnp.sum(loss, axis=0, keepdims=True) * (1.0 / TOKENS)

    def f_arrival(s):
        return remote(r.frecv.at[s], r.frecv.at[s], r.f_send.at[0, 0], r.f_recv.at[s], sib_dev)

    each(0, PL, lambda s: f_arrival(s).wait_recv())
    total = r.frecv[0].astype(F32)
    for s in range(1, PL):
        total = total + r.frecv[s].astype(F32)
    gl_out[...] = total[0:HS, :].T
    for w in range(HS // 128):
        gh_out[:, w * 128 : (w + 1) * 128] = total[HS + w * ES : HS + (w + 1) * ES, :]

    def f_sent(j):
        for c in (0, 1):

            @pl.when(jnp.logical_not(f_local(j, c)))
            def _():
                f_copy(j, c).wait_send()

    each(0, U, f_sent)


def solution(mesh):
    PL = mesh.shape["blk"]
    Z = mesh.shape["grp"] // 2
    M = 2 * Z

    def on_device(series, positives, w_last, w_head, pair_index):
        TB, D = series.shape
        HS = w_last.shape[1]
        E = w_head.shape[1]
        PT = TB // 2
        DS, ES = D // PL, E // PL
        dims = (Z, PL, TB, D, HS, E, TB * PL * M)
        pair = pair_index.reshape(M, TB)
        vm, sem = pltpu.VMEM, pltpu.SemaphoreType.DMA
        rows = M * TB
        fr = HS + ES * (HS // 128)
        scratch = dict(
            xbuf=vm((rows, D), BF16),
            wbuf=vm((D, HS), BF16),
            whbuf=vm((HS, E), BF16),
            kbuf=vm((rows, E), BF16),
            prbuf=vm((PL // 2, M, TB), jnp.int32),
            msend=vm((2, PL, PT, E), BF16),
            mrecv=vm((2, PL, PT, E), BF16),
            hidt=vm((HS, rows), BF16),
            dgt=vm((HS, rows), F32),
            hown=vm((2, Z, PT, E), F32),
            hsend=vm((2, Z, PT, E), F32),
            hsib=vm((2, Z, PT, E), F32),
            hdir=vm((2, Z, PT, E), BF16),
            hrecv=vm((2, Z, PT, E), BF16),
            ubuf=vm((2, PT, E), F32),
            rnbuf=vm((2, PT, 128), F32),
            qbuf=vm((2, PL, PT, E), BF16),
            psend=vm((2, PL, PT, E), BF16),
            precv=vm((2, PL, PT, E), BF16),
            tsend=vm((2, PL, 8, 2 * PT), F32),
            trecv=vm((2, PL, 8, 2 * PT), F32),
            gbuf=vm((rows, E), BF16),
            dpt=vm((HS, rows), BF16),
            ghb=vm((E, HS), BF16),
            fsend=vm((PL // 2, 2, fr, DS), BF16),
            frecv=vm((PL, fr, DS), BF16),
            lplane=vm((PL, 8, 128), F32),
            lcol=vm((Z, 8, 128), F32),
            lsib=vm((2, 8, 128), F32),
            x_sem=sem((2,)),
            ls_send=sem,
            ls_recv=sem,
        )
        hops = Z // 2
        sems = dict(
            w=(2,), pr=(PL // 2,), m=(2, PL), hs=(2, Z), hd=(2, Z), q=(2, PL), p=(2, PL), t=(2, PL),
            gd=(2, Z), gs=(2, Z), lp=(PL,), lc=(Z,), f=(PL // 2, 2),
        )
        for name, chunks in (("k", KEY_CHUNKS), ("a", CHUNKS[0]), ("b", CHUNKS[1])):
            sems[name] = (2, hops * chunks)
            sems[name + "s"] = (2, hops * chunks + chunks // 2)
        for name, shape in sems.items():
            scratch[name + "_send"] = sem(shape)
            scratch[name + "_recv"] = sem((PL,) if name == "f" else shape)
        names = list(scratch)

        def body(*refs):
            kernel(dims, refs[:5], refs[5:8], types.SimpleNamespace(**dict(zip(names, refs[8:]))))

        any_spec = pl.BlockSpec(memory_space=pl.ANY)
        vm_spec = pl.BlockSpec(memory_space=pltpu.VMEM)
        loss, grad_last, grad_head = pl.pallas_call(
            body,
            out_shape=(
                jax.ShapeDtypeStruct((1, 1), F32),
                jax.ShapeDtypeStruct((DS, HS), F32),
                jax.ShapeDtypeStruct((ES, HS), F32),
            ),
            in_specs=[any_spec, vm_spec, any_spec, any_spec, vm_spec],
            out_specs=(vm_spec, vm_spec, vm_spec),
            scratch_shapes=list(scratch.values()),
            compiler_params=pltpu.CompilerParams(
                collective_id=0, has_side_effects=True, vmem_limit_bytes=VMEM_BYTES
            ),
        )(series, positives, w_last, w_head, pair)
        return (loss[0, 0], grad_last, grad_head.T)

    return jax.shard_map(
        on_device,
        mesh=mesh,
        in_specs=(
            P(("blk", "grp"), None),
            P(("blk", "grp"), None),
            P(None, "grp"),
            P("grp", None),
            P("blk"),
        ),
        out_specs=(P(), P("blk", "grp"), P("grp", "blk")),
        check_vma=False,
    )
```

time: 833 us -> 144 us (0.17)
  waiting for transfers between devices: 635 us -> 0 us
  Pallas kernels: 0 us -> 139 us
  blocking collectives: 119 us -> 0 us
  matrix products: 33 us -> 0 us
  between operations: 16.1 us -> 2.41 us
  other arithmetic: 12.8 us -> 0 us
  local copies, waits for them, and re-layouts: 13.9 us -> 2.18 us
    psum x3 -> x0, waiting for transfers between devices: 426 us -> none  [the longest x1 168 us: on_device(): normalized_rows = lax.psum(partial_grad, 'grp')]
    all_gather x2 -> x0, waiting for transfers between devices: 164 us -> none  [the longest x1 139 us: on_device(): lax.all_gather(series, 'grp', axis=0, tiled=True)]
    pallas_call x0 -> x1, Pallas kernels: none -> 139 us  [on_device(): pl.pallas_call(body, out_shape=(jax.ShapeDtypeStruct((1, 1), F32), jax.Sh...]
    psum x2 -> x0, blocking collectives: 119 us -> none  [the longest x1 84.7 us: on_device(): lax.psum(jnp.sum(row_loss), ('blk', 'grp'))]
    reduce_scatter x2 -> x0, waiting for transfers between devices: 43.6 us -> none  [the longest x1 43.6 us: on_device(): lax.psum_scatter(head_partial, 'blk', scatter_dimension=1, tiled=True)]
    dot_general x12 -> x0, matrix products: 33 us -> none  [the longest x2 12.8 us: through(): lax.dot_general(left, right, (((0,), (0,)), ((), ())), preferred_element_...]
  transfers between devices with their start and end apart: 7 -> 0, of which waited for: 6 -> 0; matrix products, arithmetic and copies ran while one was open for 5% -> 0% of each run, Pallas kernels for 0% -> 0%
where the time goes in v2:
time: 144 us
  Pallas kernels  139 us (97%)
  between operations  2.41 us (2%)
  local copies, waits for them, and re-layouts  2.18 us (2%)
    pallas_call x1, Pallas kernels, on_device(): pl.pallas_call(body, out_shape=(jax.ShapeDtypeStruct((1, 1), F32), jax.Sh...  139 us

profile of v2, /device:TPU:1, one launch (start us, length us, event | category | flops | bytes accessed | tf_op | source)
XLA Modules:
  0.0 143.8 jit_solution(13607695609150857993)
XLA Ops:
  0.6 139.2 %shard_map.76 = (f32[1,1]{1,0:T(1,128)}, f32[128,256]{1,0:T(8,128)}, f32[16,256]{1,0:T(8,128)}) custom-call(bf16[128,2048]{1,0:T(8,128)(2,1)} %refs_0_.1, bf16[128,256]{1,0:T(8,128)(2,1)} %refs_1_.1, bf16[2048,256]{1,0:T(8,128)(2,1)} %refs_2_.1, bf16[256,256]{1,0:T(8,128)(2,1)} %refs_3_.1, s32[16,128]{1,0:T(8,128)} %bitcast.4), custom_call_target="tpu_custom_call" | custom-call | tf_op jit(solution)/shard_map/pallas_call | solution.py:679
  140.4 0.0 copy-start
  140.5 1.6 %copy.12 = f32[128,256]{1,0:T(8,128)} copy(f32[128,256]{1,0:T(8,128)} %get-tuple-element.13) | data formatting | bytes 262144
  142.0 0.0 copy-done
  142.0 0.6 copy.13
Async XLA Ops:
  140.4 1.6 %copy-start = (f32[16,256]{1,0:T(8,128)S(1)}, f32[16,256]{1,0:T(8,128)}, u32[]{:S(2)}) copy-start(f32[16,256]{1,0:T(8,128)} %get-tuple-element.8) | copy-start | bytes 49156

commit v3 on v2

--- a/solution.py
+++ b/solution.py
@@ -18,7 +18,9 @@
 GELU_A = math.sqrt(2.0 / math.pi)
 GELU_B = 0.044715
 KEY_CHUNKS = 2
-CHUNKS = (2, 4)
+PARTS = (64, 64)
+CHUNKS = (2, 2)
+GROUPS = (4, 4)
 VMEM_BYTES = 56 * 1024 * 1024
 
 
@@ -44,9 +46,11 @@
     r = refs
     U = PL // 2
     HOPS = Z // 2
-    PT = TB // 2
-    PART = 2 * Z * PT
-    QUAD = 4 * PT
+    K = len(PARTS)
+    first_row = [sum(PARTS[:k]) for k in range(K)]
+    part_row = [2 * Z * f for f in first_row]
+    group = GROUPS
+    g_bits = [g.bit_length() - 1 for g in group]
     KEYS = 2 * Z * TB
     DS = D // PL
     ES = E // PL
@@ -96,11 +100,14 @@
     def unit_u(j):
         return unit_of(bits_of(j, UB))
 
-    def plane(i, b=None):
+    def plane(i, b=None, low=1):
         if b is None:
-            b, i = i % 4, i // 4
-        u = unit_of([b // 2] + bits_of(i, UB - 1))
+            b, i = i % 2, i // 2
+        u = unit_of(bits_of(b // 2, low - 1) + bits_of(i, UB + 1 - low))
         return (u * 2 + core, z * 2 + flip(xhi, b % 2))
+
+    def position(i):
+        return i - 1 if 0 < i < Z - 1 else (Z - 2 if i == 0 else i)
 
     def remote(src, dst, ssem, rsem, dev):
         return pltpu.make_async_remote_copy(
@@ -113,6 +120,16 @@
             return c
 
         lax.fori_loop(low, high, step, 0)
+
+    def parts_of(name):
+        return [getattr(r, name + str(k)) for k in range(K)]
+
+    msend, mrecv, qbuf, psend, precv, tsend, trecv = map(
+        parts_of, ("msend", "mrecv", "qbuf", "psend", "precv", "tsend", "trecv")
+    )
+    hown, hsend, hsib, hdir, hrecv, ubuf, rnbuf = map(
+        parts_of, ("hown", "hsend", "hsib", "hdir", "hrecv", "ubuf", "rnbuf")
+    )
 
     barrier = pltpu.get_barrier_semaphore()
 
@@ -127,14 +144,18 @@
         greet((unit_u(i // 2) * 2 + xhi, z * 2 + flip(xhi, i % 2)))
 
     own_copies = [
-        pltpu.make_async_copy(series.at[pl.ds(k * PT, PT)], r.xbuf.at[pl.ds(k * PART, PT)], r.x_sem.at[k])
-        for k in (0, 1)
+        pltpu.make_async_copy(
+            series.at[pl.ds(first_row[k], PARTS[k])],
+            r.xbuf.at[pl.ds(part_row[k] + position(0) * 2 * PARTS[k], PARTS[k])],
+            r.x_sem.at[k],
+        )
+        for k in range(K)
     ]
     for copy in own_copies:
         copy.start()
     key_float = positives[...].astype(F32)
     key_norm = jnp.sqrt(jnp.sum(key_float * key_float, axis=1, keepdims=True) + EPSILON)
-    r.kbuf[0:TB, :] = (key_float / key_norm).astype(BF16)
+    r.kbuf[position(0) * 2 * TB : position(0) * 2 * TB + TB, :] = (key_float / key_norm).astype(BF16)
     r.prbuf[0] = pair[...]
 
     pl.semaphore_wait(barrier, 1 + (Z - 1) + (PL - 1) + PL - 2 * jnp.where(holder, 1, 0))
@@ -156,7 +177,7 @@
 
         def at(self, i, rel, chunk, count=1):
             size = self.rows // self.chunks
-            return self.buf.at[pl.ds(self.base + (i * 2 + rel) * self.rows + chunk * size, size * count)]
+            return self.buf.at[pl.ds(self.base + (position(i) * 2 + rel) * self.rows + chunk * size, size * count)]
 
         def send(self, direction, hop, chunk):
             size = self.rows // self.chunks
@@ -194,10 +215,13 @@
                 src, self.at(0, 1, 0, self.chunks), self.sems[2].at[0, last], self.sems[3].at[0, last], sib_dev
             )
 
+        def begin_with(self, n):
+            for direction in (0, 1):
+                self.send(direction, 0, self.chunk_list(direction, 0)[n]).start()
+
         def begin(self):
-            for a, b in zip(self.chunk_list(0, 0), self.chunk_list(1, 0)):
-                self.send(0, 0, a).start()
-                self.send(1, 0, b).start()
+            for n in range(self.chunks):
+                self.begin_with(n)
             self.over_own().start()
 
         def passing(self, hop, n):
@@ -231,10 +255,11 @@
 
     keys_ring = Ring("k", r.kbuf, 0, TB, KEY_CHUNKS, None)
     rings = [
-        Ring("ab"[k], r.xbuf, k * PART, PT, CHUNKS[k], series.at[pl.ds(k * PT, PT)]) for k in (0, 1)
+        Ring("x%d" % k, r.xbuf, part_row[k], PARTS[k], CHUNKS[k], series.at[pl.ds(first_row[k], PARTS[k])])
+        for k in range(K)
     ]
     keys_ring.begin()
-    rings[0].begin()
+    rings[0].begin_with(0)
 
     partner = (blk, z * 2 + 1 - xhi)
     w_copies = [
@@ -256,128 +281,141 @@
         pair_copy(j).start()
 
     class Swap:
-        def __init__(self, name, src, dst, part):
-            self.src, self.dst = src.at[part], dst.at[part]
-            self.ssem, self.rsem = (getattr(r, name + s).at[part] for s in ("_send", "_recv"))
-
-        def copy(self, i, b=None):
-            k = i if b is None else i * 4 + b
-            return remote(self.src.at[k], self.dst.at[k], self.ssem.at[k], self.rsem.at[k], plane(i, b))
+        def __init__(self, name, src, dst, k):
+            self.src, self.dst, self.k = getattr(r, src + str(k)), getattr(r, dst + str(k)), k
+            self.ssem, self.rsem = (getattr(r, name + s).at[k] for s in ("_send", "_recv"))
+
+        def copy(self, i, b=None, own=False):
+            k = i if b is None else i * group[self.k] + b
+            dev = plane(i) if b is None else plane(i, b, g_bits[self.k])
+            src = self.src.at[0 if own else k]
+            return remote(src, self.dst.at[k], self.ssem.at[k], self.rsem.at[k], dev)
 
         def own_copy(self, i, b=None):
-            k = i if b is None else i * 4 + b
-            return remote(self.src.at[0], self.dst.at[k], self.ssem.at[k], self.rsem.at[k], plane(i, b))
-
-    swap_m = [Swap("m", r.msend, r.mrecv, k) for k in (0, 1)]
-    swap_q = [Swap("q", r.qbuf, r.qbuf, k) for k in (0, 1)]
-    swap_p = [Swap("p", r.psend, r.precv, k) for k in (0, 1)]
-    swap_t = [Swap("t", r.tsend, r.trecv, k) for k in (0, 1)]
-
-    def quad(u, body):
-        for b in range(4):
+            return self.copy(i, b, True)
+
+    swap_m = [Swap("m", "msend", "mrecv", k) for k in range(K)]
+    swap_q = [Swap("q", "qbuf", "qbuf", k) for k in range(K)]
+    swap_p = [Swap("p", "psend", "precv", k) for k in range(K)]
+    swap_t = [Swap("t", "tsend", "trecv", k) for k in range(K)]
+
+    def members(k, u, body):
+        for b in range(group[k]):
             if b == 0:
                 pl.when(u != 0)(functools.partial(body, u, b))
             else:
                 body(u, b)
 
-    def find_pairs(k):
+    def find_pairs(k, low, high):
+        n, g = PARTS[k], group[k]
+        UNIT = n * g
+
         def unit(u):
-            lanes = lax.broadcasted_iota(jnp.int32, (QUAD, TB), 1)
+            lanes = lax.broadcasted_iota(jnp.int32, (UNIT, TB), 1)
             cols = []
-            for b in range(4):
-                row = r.prbuf[u * 2 + b // 2, pl.ds(z * 2 + flip(xhi, b % 2), 1), :]
-                cols.append(jnp.broadcast_to(row, (TB, TB)).T[k * PT : (k + 1) * PT, :])
+            for b in range(g):
+                row = r.prbuf[u * (g // 2) + b // 2, pl.ds(z * 2 + flip(xhi, b % 2), 1), :]
+                cols.append(jnp.broadcast_to(row, (TB, TB)).T[first_row[k] : first_row[k] + n, :])
             both = jnp.concatenate(cols, axis=0) - lanes
-            total = jnp.zeros((QUAD, E), F32)
+            total = jnp.zeros((UNIT, E), F32)
             for i in range(Z):
-                low = (unit_z(i) * 2 + xhi) * TB
-                hot = jnp.concatenate([both == blk * GRP_ROWS + low, both == sib_blk * GRP_ROWS + low], axis=1)
+                base = (unit_z(i) * 2 + xhi) * TB
+                hot = jnp.concatenate([both == blk * GRP_ROWS + base, both == sib_blk * GRP_ROWS + base], axis=1)
                 hot = jnp.where(hot, 1.0, 0.0).astype(BF16)
-                total = total + dot_nn(hot, r.kbuf[i * 2 * TB : (i + 1) * 2 * TB, :])
-            for b in range(4):
-                r.msend[k, u * 4 + b] = total[b * PT : (b + 1) * PT, :].astype(BF16)
-            quad(u, lambda *at: swap_m[k].copy(*at).start())
-
-        each(0, PL // 4, unit)
-
-    def block(hop):
-        return (0, 1) if hop == 0 else (2 * hop - 1, min(2 * hop + 1, Z))
+                at = position(i) * 2 * TB
+                total = total + dot_nn(hot, r.kbuf[at : at + 2 * TB, :])
+            for b in range(g):
+                msend[k][u * g + b] = total[b * n : (b + 1) * n, :].astype(BF16)
+            members(k, u, lambda *at: swap_m[k].copy(*at).start())
+
+        each(low, high, unit)
+
+    def places(hops):
+        out = []
+        for hop in hops:
+            out += [0] if hop == 0 else ([Z - 1] if hop == HOPS else [2 * hop - 1, 2 * hop])
+        return out
+
+    def span(k, hops):
+        at = [position(i) for i in places(hops)]
+        return part_row[k] + at[0] * 2 * PARTS[k], part_row[k] + (at[-1] + 1) * 2 * PARTS[k]
 
     def hs_copy(k, i):
-        return remote(r.hsend.at[k, i], r.hsib.at[k, i], r.hs_send.at[k, i], r.hs_recv.at[k, i], sib_dev)
+        return remote(hsend[k].at[i], hsib[k].at[i], r.hs_send.at[k, i], r.hs_recv.at[k, i], sib_dev)
 
     def hd_copy(k, i):
         slot = seen_from(i)
-        return remote(r.hdir.at[k, i], r.hrecv.at[k, slot], r.hd_send.at[k, i], r.hd_recv.at[k, slot], column(i))
-
-    def encode(k, hop):
-        rings[k].other_ready(hop)
-        low, high = block(hop)
-        start, stop = k * PART + low * 2 * PT, k * PART + high * 2 * PT
+        return remote(hdir[k].at[i], hrecv[k].at[slot], r.hd_send.at[k, i], r.hd_recv.at[k, slot], column(i))
+
+    def encode(k, *hops):
+        n = PARTS[k]
+        for hop in hops:
+            rings[k].other_ready(hop)
+        start, stop = span(k, hops)
         x = dot_nn(r.xbuf[start:stop, :], r.wbuf[...])
         x2 = x * x
         t = jnp.tanh(GELU_A * (x + GELU_B * (x2 * x)))
         cdf = 0.5 + 0.5 * t
         hidden = x * cdf
         out = dot_nn(hidden.astype(BF16), r.whbuf[...])
-        for i in range(low, high):
-            first = (i - low) * 2 * PT
-            r.hown[k, i] = out[first : first + PT, :]
-            r.hsend[k, i] = out[first + PT : first + 2 * PT, :]
+        for m, i in enumerate(places(hops)):
+            hown[k][i] = out[m * 2 * n : m * 2 * n + n, :]
+            hsend[k][i] = out[m * 2 * n + n : (m + 1) * 2 * n, :]
             hs_copy(k, i).start()
         r.hidt[:, start:stop] = hidden.T.astype(BF16)
         dgelu = cdf + (0.5 * GELU_A) * x * (1.0 - t * t) * (1.0 + (3.0 * GELU_B) * x2)
         r.dgt[:, start:stop] = dgelu.T
 
-    def head_send(k, hop):
-        for i in range(*block(hop)):
+    def head_send(k, *hops):
+        for i in places(hops):
             if i:
                 hs_copy(k, i).wait_recv()
-                r.hdir[k, i] = (r.hown[k, i] + r.hsib[k, i]).astype(BF16)
+                hdir[k][i] = (hown[k][i] + hsib[k][i]).astype(BF16)
                 hd_copy(k, i).start()
 
     def make_queries(k):
         hs_copy(k, 0).wait_recv()
-        head = r.hown[k, 0] + r.hsib[k, 0]
+        head = hown[k][0] + hsib[k][0]
         for i in range(1, Z):
             hd_copy(k, seen_from(i)).wait_recv()
-            head = head + r.hrecv[k, i].astype(F32)
+            head = head + hrecv[k][i].astype(F32)
         row_norm = jnp.sqrt(jnp.sum(head * head, axis=1, keepdims=True) + EPSILON)
         unit_rows = head / row_norm
-        r.ubuf[k] = unit_rows
-        r.rnbuf[k] = jnp.broadcast_to(row_norm, (PT, 128))
-        r.qbuf[k, 0] = unit_rows.astype(BF16)
+        ubuf[k][...] = unit_rows
+        rnbuf[k][...] = jnp.broadcast_to(row_norm, (PARTS[k], 128))
+        qbuf[k][0] = unit_rows.astype(BF16)
         for i in range(1, PL):
             swap_q[k].own_copy(i).start()
 
     CHUNK = min(512, KEYS)
     scale = (1.0 / TEMP) * math.log2(math.e)
 
-    def attend(k):
+    def attend(k, low, high):
+        n, g = PARTS[k], group[k]
+        UNIT = n * g
+
         def unit(u):
-            quad(u, lambda *at: swap_q[k].own_copy(*at).wait_recv())
-            q = r.qbuf[k, pl.ds(u * 4, 4)].reshape(QUAD, E)
-            total = jnp.zeros((QUAD, 128), F32)
-            weighted = jnp.zeros((QUAD, E), F32)
+            members(k, u, lambda *at: swap_q[k].own_copy(*at).wait_recv())
+            q = qbuf[k][pl.ds(u * g, g)].reshape(UNIT, E)
+            total = jnp.zeros((UNIT, 128), F32)
+            weighted = jnp.zeros((UNIT, E), F32)
             for c in range(KEYS // CHUNK):
                 keys = r.kbuf[c * CHUNK : (c + 1) * CHUNK, :]
                 e = jnp.exp2(dot_nt(q, keys) * scale)
                 total = total + fold_lanes(e)
                 weighted = weighted + dot_nn(e.astype(BF16), keys)
-            for b in range(4):
-                r.psend[k, u * 4 + b] = weighted[b * PT : (b + 1) * PT, :].astype(BF16)
-            for b in (0, 1):
-                part = jnp.sum(total[b * 2 * PT : (b + 1) * 2 * PT, :].T, axis=0, keepdims=True)
-                part = jnp.broadcast_to(part, (8, 2 * PT))
-                r.tsend[k, u * 4 + b * 2] = part
-                r.tsend[k, u * 4 + b * 2 + 1] = part
-            quad(u, lambda *at: swap_p[k].copy(*at).start())
-            quad(u, lambda *at: swap_t[k].copy(*at).start())
-
-        each(0, PL // 4, unit)
+            for b in range(g):
+                psend[k][u * g + b] = weighted[b * n : (b + 1) * n, :].astype(BF16)
+            members(k, u, lambda *at: swap_p[k].copy(*at).start())
+            part = jnp.sum(total.T, axis=0, keepdims=True)
+            for b in range(g):
+                tsend[k][u * g + b] = part
+            members(k, u, lambda *at: swap_t[k].copy(*at).start())
+
+        each(low, high, unit)
 
     def g_rows(k, i, rel):
-        return r.gbuf.at[pl.ds(k * PART + (i * 2 + rel) * PT, PT)]
+        return r.gbuf.at[pl.ds(part_row[k] + (position(i) * 2 + rel) * PARTS[k], PARTS[k])]
 
     def g_direct(k, i):
         slot = seen_from(i)
@@ -391,46 +429,50 @@
         return remote(g_rows(k, i, rel), g_rows(k, i, 1), r.gs_send.at[k, i], r.gs_recv.at[k, i], sib_dev)
 
     def make_rows(k):
-        matched = r.msend[k, 0].astype(F32)
+        n, g = PARTS[k], group[k]
+        UNIT = n * g
+        matched = msend[k][0].astype(F32)
         for i in range(1, PL):
             swap_m[k].copy(i).wait_recv()
-            matched = matched + r.mrecv[k, i].astype(F32)
-        weighted = r.psend[k, 0].astype(F32)
-        totals = [r.tsend[k, 0], jnp.zeros((8, 2 * PT), F32)]
+            matched = matched + mrecv[k][i].astype(F32)
+        weighted = psend[k][0].astype(F32)
+        lanes = lax.broadcasted_iota(jnp.int32, (1, UNIT), 1)
+        side = [jnp.logical_and(lanes >= b * n, lanes < (b + 1) * n) for b in range(g)]
+        totals = jnp.where(side[0], tsend[k][0], 0.0)
         for i in range(1, PL):
             swap_p[k].copy(i).wait_recv()
             swap_t[k].copy(i).wait_recv()
-            weighted = weighted + r.precv[k, i].astype(F32)
-            totals[i % 2] = totals[i % 2] + r.trecv[k, i]
-        sides = [jnp.broadcast_to(totals[b][0:1, :], (128, 2 * PT)).T for b in (0, 1)]
-        total = sides[0][0:PT, :] + sides[1][PT : 2 * PT, :]
+            weighted = weighted + precv[k][i].astype(F32)
+            totals = totals + jnp.where(side[i % g], trecv[k][i], 0.0)
+        column_totals = jnp.broadcast_to(totals, (128, UNIT)).T
+        total = column_totals[0:n, :]
+        for b in range(1, g):
+            total = total + column_totals[b * n : (b + 1) * n, :]
         wide = jnp.concatenate([total] * (E // 128), axis=1)
         grad = (weighted / wide - matched) * (1.0 / TEMP)
-        unit_rows = r.ubuf[k]
+        unit_rows = ubuf[k][...]
         along = jnp.sum(unit_rows * grad, axis=1, keepdims=True)
-        norm = jnp.concatenate([r.rnbuf[k]] * (E // 128), axis=1)
-        r.gbuf[k * PART : k * PART + PT, :] = ((grad - unit_rows * along) / norm).astype(BF16)
+        norm = jnp.concatenate([rnbuf[k][...]] * (E // 128), axis=1)
+        g_rows(k, 0, 0)[...] = ((grad - unit_rows * along) / norm).astype(BF16)
         g_over(k, 0).start()
         for i in range(1, Z):
             g_direct(k, i).start()
-        hit = r.qbuf[k, 0].astype(F32) * matched
-        hit = fold_lanes(jnp.sum(hit.reshape(PT // 8, 8, E), axis=0))
-        logs = jnp.sum(jnp.log(total).reshape(PT // 8, 8, 128), axis=0)
+        hit = qbuf[k][0].astype(F32) * matched
+        hit = fold_lanes(jnp.sum(hit.reshape(n // 8, 8, E), axis=0))
+        logs = jnp.sum(jnp.log(total).reshape(n // 8, 8, 128), axis=0)
         first = lax.broadcasted_iota(jnp.int32, (8, 128), 1) == 0
         return jnp.where(first, logs, 0.0) - hit * (1.0 / TEMP)
 
-    def back(k):
-        for hop in range(HOPS + 1):
-            low, high = block(hop)
-            for i in range(low, high):
-                if i:
-                    g_arrival(k, i).wait_recv()
-                    g_over(k, i).start()
-            for i in range(low, high):
-                g_over(k, i, 1).wait_recv()
-            start, stop = k * PART + low * 2 * PT, k * PART + high * 2 * PT
-            dp = dot_nt(r.whbuf[...], r.gbuf[start:stop, :]) * r.dgt[:, start:stop]
-            r.dpt[:, start:stop] = dp.astype(BF16)
+    def back(k, *hops):
+        for i in places(hops):
+            if i:
+                g_arrival(k, i).wait_recv()
+                g_over(k, i).start()
+        for i in places(hops):
+            g_over(k, i, 1).wait_recv()
+        start, stop = span(k, hops)
+        dp = dot_nt(r.whbuf[...], r.gbuf[start:stop, :]) * r.dgt[:, start:stop]
+        r.dpt[:, start:stop] = dp.astype(BF16)
 
     def lp_copy(i):
         return remote(r.lplane.at[pid], r.lplane.at[pid], r.lp_send.at[i], r.lp_recv.at[i], plane(i))
@@ -452,52 +494,58 @@
 
     for copy in own_copies:
         copy.wait()
-    for hop in range(1, HOPS):
-        keys_ring.passing_all(hop)
-        rings[0].passing_all(hop)
+    keys_ring.passing_all(1)
+    rings[0].begin_with(1)
+    rings[0].over_own().start()
+    keys_ring.passing_all(2)
+    rings[0].passing(1, 0)
+    keys_ring.passing_all(3)
+    rings[0].passing(1, 1)
+    keys_ring.passing_all(4)
+    rings[0].passing(2, 0)
+    for j in range(1, U):
+        pair_copy(j).wait_recv()
+    for hop in range(HOPS + 1):
+        keys_ring.other_ready(hop)
+    find_pairs(0, 0, 2)
+    rings[0].passing(2, 1)
+    find_pairs(0, 2, 4)
+    rings[0].passing(3, 0)
+    find_pairs(1, 0, 2)
+    rings[0].passing(3, 1)
     rings[1].begin()
+    find_pairs(1, 2, 4)
     for copy in w_copies:
         copy.wait_recv()
-    for hop in range(HOPS - 1):
-        encode(0, hop)
-    for j in range(1, U):
-        pair_copy(j).wait_recv()
-    keys_ring.passing_all(HOPS)
-    rings[0].passing_all(HOPS)
-    encode(0, HOPS - 1)
-    encode(0, HOPS)
-    for hop in range(1, HOPS - 1):
-        head_send(0, hop)
-    rings[1].passing(1, 0)
-    head_send(0, HOPS - 1)
-    head_send(0, HOPS)
-    for n in range(1, CHUNKS[1]):
-        rings[1].passing(1, n)
-    for hop in range(HOPS + 1):
-        keys_ring.other_ready(hop)
-    find_pairs(0)
+    encode(0, 1)
+    encode(0, 2)
+    rings[0].passing_all(4)
+    encode(0, 3)
+    head_send(0, 1, 2)
+    encode(0, 0, 4)
+    head_send(0, 3, 0, 4)
+    rings[1].passing_all(1)
     rings[1].passing_all(2)
+    encode(1, 1)
+    rings[1].passing_all(3)
+    encode(1, 2)
     make_queries(0)
-    find_pairs(1)
-    rings[1].passing_all(3)
-    encode(1, 0)
-    attend(0)
-    encode(1, 1)
     rings[1].passing_all(4)
-    encode(1, 2)
     encode(1, 3)
-    encode(1, 4)
-    for hop in range(1, HOPS + 1):
-        head_send(1, hop)
+    encode(1, 0, 4)
+    head_send(1, 1, 2, 3, 0, 4)
+    attend(0, 0, 4)
+    make_queries(1)
     loss = make_rows(0)
-    make_queries(1)
-    back(0)
-    attend(1)
+    attend(1, 0, 4)
+    back(0, 1, 2)
+    back(0, 3, 0, 4)
     loss = loss + make_rows(1)
     r.lplane[pid] = loss
     for i in range(1, PL):
         lp_copy(i).start()
-    back(1)
+    back(1, 1, 2)
+    back(1, 3, 0, 4)
 
     ghead = dot_nn(r.hidt[...], r.gbuf[...])
     r.ghb[...] = ghead.T.astype(BF16)
@@ -564,7 +612,7 @@
 
     for j in range(1, U):
         pair_copy(j).wait_send()
-    for k in (0, 1):
+    for k in range(K):
         for i in range(Z):
             hs_copy(k, i).wait_send()
             g_over(k, i).wait_send()
@@ -612,12 +660,12 @@
     PL = mesh.shape["blk"]
     Z = mesh.shape["grp"] // 2
     M = 2 * Z
+    K = len(PARTS)
 
     def on_device(series, positives, w_last, w_head, pair_index):
         TB, D = series.shape
         HS = w_last.shape[1]
         E = w_head.shape[1]
-        PT = TB // 2
         DS, ES = D // PL, E // PL
         dims = (Z, PL, TB, D, HS, E, TB * PL * M)
         pair = pair_index.reshape(M, TB)
@@ -630,22 +678,8 @@
             whbuf=vm((HS, E), BF16),
             kbuf=vm((rows, E), BF16),
             prbuf=vm((PL // 2, M, TB), jnp.int32),
-            msend=vm((2, PL, PT, E), BF16),
-            mrecv=vm((2, PL, PT, E), BF16),
             hidt=vm((HS, rows), BF16),
             dgt=vm((HS, rows), F32),
-            hown=vm((2, Z, PT, E), F32),
-            hsend=vm((2, Z, PT, E), F32),
-            hsib=vm((2, Z, PT, E), F32),
-            hdir=vm((2, Z, PT, E), BF16),
-            hrecv=vm((2, Z, PT, E), BF16),
-            ubuf=vm((2, PT, E), F32),
-            rnbuf=vm((2, PT, 128), F32),
-            qbuf=vm((2, PL, PT, E), BF16),
-            psend=vm((2, PL, PT, E), BF16),
-            precv=vm((2, PL, PT, E), BF16),
-            tsend=vm((2, PL, 8, 2 * PT), F32),
-            trecv=vm((2, PL, 8, 2 * PT), F32),
             gbuf=vm((rows, E), BF16),
             dpt=vm((HS, rows), BF16),
             ghb=vm((E, HS), BF16),
@@ -654,16 +688,27 @@
             lplane=vm((PL, 8, 128), F32),
             lcol=vm((Z, 8, 128), F32),
             lsib=vm((2, 8, 128), F32),
-            x_sem=sem((2,)),
+            x_sem=sem((K,)),
             ls_send=sem,
             ls_recv=sem,
         )
+        for k, n in enumerate(PARTS):
+            for name in ("msend", "mrecv", "qbuf", "psend", "precv"):
+                scratch[name + str(k)] = vm((PL, n, E), BF16)
+            for name in ("tsend", "trecv"):
+                scratch[name + str(k)] = vm((PL, 1, n * GROUPS[k]), F32)
+            for name in ("hown", "hsend", "hsib"):
+                scratch[name + str(k)] = vm((Z, n, E), F32)
+            for name in ("hdir", "hrecv"):
+                scratch[name + str(k)] = vm((Z, n, E), BF16)
+            scratch["ubuf" + str(k)] = vm((n, E), F32)
+            scratch["rnbuf" + str(k)] = vm((n, 128), F32)
         hops = Z // 2
         sems = dict(
-            w=(2,), pr=(PL // 2,), m=(2, PL), hs=(2, Z), hd=(2, Z), q=(2, PL), p=(2, PL), t=(2, PL),
-            gd=(2, Z), gs=(2, Z), lp=(PL,), lc=(Z,), f=(PL // 2, 2),
+            w=(2,), pr=(PL // 2,), m=(K, PL), hs=(K, Z), hd=(K, Z), q=(K, PL), p=(K, PL), t=(K, PL),
+            gd=(K, Z), gs=(K, Z), lp=(PL,), lc=(Z,), f=(PL // 2, 2),
         )
-        for name, chunks in (("k", KEY_CHUNKS), ("a", CHUNKS[0]), ("b", CHUNKS[1])):
+        for name, chunks in [("k", KEY_CHUNKS)] + [("x%d" % k, c) for k, c in enumerate(CHUNKS)]:
             sems[name] = (2, hops * chunks)
             sems[name + "s"] = (2, hops * chunks + chunks // 2)
         for name, shape in sems.items():

time: 144 us -> 135 us (0.938)
  Pallas kernels: 139 us -> 130 us
    pallas_call x1, Pallas kernels: 139 us -> 130 us  [on_device(): pl.pallas_call(body, out_shape=(jax.ShapeDtypeStruct((1, 1), F32), jax.Sh...]
where the time goes in v3:
time: 135 us
  Pallas kernels  130 us (96%)
  between operations  2.41 us (2%)
  local copies, waits for them, and re-layouts  2.18 us (2%)
    pallas_call x1, Pallas kernels, on_device(): pl.pallas_call(body, out_shape=(jax.ShapeDtypeStruct((1, 1), F32), jax.Sh...  130 us

profile of v3, /device:TPU:1, one launch (start us, length us, event | category | flops | bytes accessed | tf_op | source)
XLA Modules:
  0.0 134.6 jit_solution(14961959339505666496)
XLA Ops:
  0.6 130.0 %shard_map.76 = (f32[1,1]{1,0:T(1,128)}, f32[128,256]{1,0:T(8,128)}, f32[16,256]{1,0:T(8,128)}) custom-call(bf16[128,2048]{1,0:T(8,128)(2,1)} %refs_0_.1, bf16[128,256]{1,0:T(8,128)(2,1)} %refs_1_.1, bf16[2048,256]{1,0:T(8,128)(2,1)} %refs_2_.1, bf16[256,256]{1,0:T(8,128)(2,1)} %refs_3_.1, s32[16,128]{1,0:T(8,128)} %bitcast.4), custom_call_target="tpu_custom_call" | custom-call | tf_op jit(solution)/shard_map/pallas_call | solution.py:724
  131.3 0.0 copy-start
  131.3 1.6 %copy.12 = f32[128,256]{1,0:T(8,128)} copy(f32[128,256]{1,0:T(8,128)} %get-tuple-element.13) | data formatting | bytes 262144
  132.9 0.0 copy-done
  132.9 0.6 copy.13
Async XLA Ops:
  131.3 1.6 %copy-start = (f32[16,256]{1,0:T(8,128)S(1)}, f32[16,256]{1,0:T(8,128)}, u32[]{:S(2)}) copy-start(f32[16,256]{1,0:T(8,128)} %get-tuple-element.8) | copy-start | bytes 49156

commit v4 on v3

--- a/solution.py
+++ b/solution.py
@@ -42,7 +42,7 @@
 def kernel(dims, refs_in, refs_out, refs):
     Z, PL, TB, D, HS, E, TOKENS = dims
     series, positives, w_last, w_head, pair = refs_in
-    loss_out, gl_out, gh_out = refs_out
+    (sums_out,) = refs_out
     r = refs
     U = PL // 2
     HOPS = Z // 2
@@ -633,7 +633,9 @@
     ls_copy(core).wait_send()
     loss = r.lsib[0] + r.lsib[1]
     loss = jnp.sum(loss, axis=1, keepdims=True)
-    loss_out[...] = jnp.sum(loss, axis=0, keepdims=True) * (1.0 / TOKENS)
+    loss = jnp.sum(loss, axis=0, keepdims=True) * (1.0 / TOKENS)
+    sums = HS + ES * (HS // 128)
+    sums_out[sums : sums + 8, :] = jnp.broadcast_to(loss, (8, DS))
 
     def f_arrival(s):
         return remote(r.frecv.at[s], r.frecv.at[s], r.f_send.at[0, 0], r.f_recv.at[s], sib_dev)
@@ -642,9 +644,7 @@
     total = r.frecv[0].astype(F32)
     for s in range(1, PL):
         total = total + r.frecv[s].astype(F32)
-    gl_out[...] = total[0:HS, :].T
-    for w in range(HS // 128):
-        gh_out[:, w * 128 : (w + 1) * 128] = total[HS + w * ES : HS + (w + 1) * ES, :]
+    sums_out[0:sums, :] = total
 
     def f_sent(j):
         for c in (0, 1):
@@ -654,6 +654,15 @@
                 f_copy(j, c).wait_send()
 
     each(0, U, f_sent)
+
+
+def finish(sums, loss_out, gl_out, gh_out):
+    HS, (ES, _) = gl_out.shape[1], gh_out.shape
+    gl_out[...] = sums[0:HS, :].T
+    for w in range(HS // 128):
+        gh_out[:, w * 128 : (w + 1) * 128] = sums[HS + w * ES : HS + (w + 1) * ES, :]
+    end = HS + ES * (HS // 128)
+    loss_out[...] = sums[end : end + 1, 0:1]
 
 
 def solution(mesh):
@@ -717,24 +726,30 @@
         names = list(scratch)
 
         def body(*refs):
-            kernel(dims, refs[:5], refs[5:8], types.SimpleNamespace(**dict(zip(names, refs[8:]))))
+            kernel(dims, refs[:5], refs[5:6], types.SimpleNamespace(**dict(zip(names, refs[6:]))))
 
         any_spec = pl.BlockSpec(memory_space=pl.ANY)
         vm_spec = pl.BlockSpec(memory_space=pltpu.VMEM)
+        (sums,) = pl.pallas_call(
+            body,
+            out_shape=(pltpu.VMEM((fr + 8, DS), F32),),
+            in_specs=[any_spec, vm_spec, any_spec, any_spec, vm_spec],
+            out_specs=(vm_spec,),
+            scratch_shapes=list(scratch.values()),
+            compiler_params=pltpu.CompilerParams(
+                collective_id=0, has_side_effects=True, vmem_limit_bytes=VMEM_BYTES
+            ),
+        )(series, positives, w_last, w_head, pair)
         loss, grad_last, grad_head = pl.pallas_call(
-            body,
+            finish,
             out_shape=(
                 jax.ShapeDtypeStruct((1, 1), F32),
                 jax.ShapeDtypeStruct((DS, HS), F32),
                 jax.ShapeDtypeStruct((ES, HS), F32),
             ),
-            in_specs=[any_spec, vm_spec, any_spec, any_spec, vm_spec],
+            in_specs=[vm_spec],
             out_specs=(vm_spec, vm_spec, vm_spec),
-            scratch_shapes=list(scratch.values()),
-            compiler_params=pltpu.CompilerParams(
-                collective_id=0, has_side_effects=True, vmem_limit_bytes=VMEM_BYTES
-            ),
-        )(series, positives, w_last, w_head, pair)
+        )(sums)
         return (loss[0, 0], grad_last, grad_head.T)
 
     return jax.shard_map(

time: 135 us -> 133 us (0.985)
  between operations: 2.41 us -> 0.65 us
  local copies, waits for them, and re-layouts: 2.18 us -> 0.64 us
    unnamed x4 -> x2, local copies, waits for them, and re-layouts: 2.18 us -> 0.64 us
    pallas_call x1 -> x2, Pallas kernels: 130 us -> 131 us  [the longest x1 130 us: on_device(): pl.pallas_call(body, out_shape=(pltpu.VMEM((fr + 8, DS), F32),), in_specs...]
where the time goes in v4:
time: 133 us
  Pallas kernels  131 us (98%)
    pallas_call x1, Pallas kernels, on_device(): pl.pallas_call(body, out_shape=(pltpu.VMEM((fr + 8, DS), F32),), in_specs...  130 us

profile of v4, /device:TPU:1, one launch (start us, length us, event | category | flops | bytes accessed | tf_op | source)
XLA Modules:
  0.0 132.8 jit_solution(14198151325158689340)
XLA Ops:
  0.6 129.8 %shard_map.76.sums = f32[296,128]{1,0:T(8,128)S(1)} custom-call(bf16[128,2048]{1,0:T(8,128)(2,1)} %refs_0_.1, bf16[128,256]{1,0:T(8,128)(2,1)} %refs_1_.1, bf16[2048,256]{1,0:T(8,128)(2,1)} %refs_2_.1, bf16[256,256]{1,0:T(8,128)(2,1)} %refs_3_.1, s32[16,128]{1,0:T(8,128)} %bitcast.3), custom_call_target="tpu_custom_call" | custom-call | tf_op jit(solution)/shard_map/pallas_call | solution.py:733
  130.5 0.0 copy-start
  130.5 0.6 copy-done
  131.1 1.7 %shard_map.77 = (f32[1,1]{1,0:T(1,128)}, f32[128,256]{1,0:T(8,128)}, f32[16,256]{1,0:T(8,128)}) custom-call(f32[296,128]{1,0:T(8,128)} %copy-done), custom_call_target="tpu_custom_call" | custom-call | tf_op jit(solution)/shard_map/pallas_call | solution.py:743
Async XLA Ops:
  130.5 0.7 copy-start

commit v5 on v4

--- a/solution.py
+++ b/solution.py
@@ -540,6 +540,7 @@
     attend(1, 0, 4)
     back(0, 1, 2)
     back(0, 3, 0, 4)
+    ghead = dot_nn(r.hidt[:, 0 : part_row[1]], r.gbuf[0 : part_row[1], :])
     loss = loss + make_rows(1)
     r.lplane[pid] = loss
     for i in range(1, PL):
@@ -547,17 +548,8 @@
     back(1, 1, 2)
     back(1, 3, 0, 4)
 
-    ghead = dot_nn(r.hidt[...], r.gbuf[...])
+    ghead = ghead + dot_nn(r.hidt[:, part_row[1] :], r.gbuf[part_row[1] :, :])
     r.ghb[...] = ghead.T.astype(BF16)
-
-    for i in range(1, PL):
-        lp_arrival(i).wait_recv()
-    loss = r.lplane[0]
-    for p in range(1, PL):
-        loss = loss + r.lplane[p]
-    r.lcol[z] = loss
-    for i in range(1, Z):
-        lc_copy(i).start()
 
     def f_copy(j, c):
         slot = j * 2 + jnp.where(holder, 0, 1)
@@ -594,13 +586,14 @@
 
     each(0, U, last)
 
+    for i in range(1, PL):
+        lp_arrival(i).wait_recv()
+    loss = r.lplane[0]
+    for p in range(1, PL):
+        loss = loss + r.lplane[p]
+    r.lcol[z] = loss
     for i in range(1, Z):
-        lc_arrival(i).wait_recv()
-    loss = r.lcol[0]
-    for p in range(1, Z):
-        loss = loss + r.lcol[p]
-    r.lsib[core] = loss
-    ls_copy(core).start()
+        lc_copy(i).start()
 
     for ring in [keys_ring] + rings:
         ring.drain()
@@ -624,6 +617,13 @@
             swap_m[k].copy(i).wait_send()
             swap_p[k].copy(i).wait_send()
             swap_t[k].copy(i).wait_send()
+    for i in range(1, Z):
+        lc_arrival(i).wait_recv()
+    loss = r.lcol[0]
+    for p in range(1, Z):
+        loss = loss + r.lcol[p]
+    r.lsib[core] = loss
+    ls_copy(core).start()
     for i in range(1, PL):
         lp_copy(i).wait_send()
     for i in range(1, Z):

time: 133 us -> 133 us (level)
  no operation moved by 1% of the time
where the time goes in v5:
time: 133 us
  Pallas kernels  131 us (98%)
    pallas_call x1, Pallas kernels, on_device(): pl.pallas_call(body, out_shape=(pltpu.VMEM((fr + 8, DS), F32),), in_specs...  130 us

profile of v5, /device:TPU:1, one launch (start us, length us, event | category | flops | bytes accessed | tf_op | source)
XLA Modules:
  0.0 132.7 jit_solution(9870409297145824949)
XLA Ops:
  0.6 129.7 %shard_map.76.sums = f32[296,128]{1,0:T(8,128)S(1)} custom-call(bf16[128,2048]{1,0:T(8,128)(2,1)} %refs_0_.1, bf16[128,256]{1,0:T(8,128)(2,1)} %refs_1_.1, bf16[2048,256]{1,0:T(8,128)(2,1)} %refs_2_.1, bf16[256,256]{1,0:T(8,128)(2,1)} %refs_3_.1, s32[16,128]{1,0:T(8,128)} %bitcast.3), custom_call_target="tpu_custom_call" | custom-call | tf_op jit(solution)/shard_map/pallas_call | solution.py:733
  130.4 0.0 copy-start
  130.4 0.6 copy-done
  131.0 1.7 %shard_map.77 = (f32[1,1]{1,0:T(1,128)}, f32[128,256]{1,0:T(8,128)}, f32[16,256]{1,0:T(8,128)}) custom-call(f32[296,128]{1,0:T(8,128)} %copy-done), custom_call_target="tpu_custom_call" | custom-call | tf_op jit(solution)/shard_map/pallas_call | solution.py:743
Async XLA Ops:
  130.4 0.7 copy-start
